TPU v7x, 128 devices: a whole 4x4x4 slice. The times are simulated.
128 devices in a mesh: tok: 8 (over x, y_hi), voc: 16 (over y_lo, z, core).
Axes of the slice: x: 4, y: 4 (y_hi: 2, y_lo: 2; y = y_hi * 2 + y_lo), z: 4, core: 2. Of those that a mesh axis runs over, the one named last changes fastest.
Arguments:
- teacher_hidden: bfloat16 [256, 4096], P(None, 'tok'), may hold values from -70 to 70
- teacher_head: bfloat16 [4096, 8, 12288], P('tok', None, 'voc')
- student_hidden: bfloat16 [256, 2, 2560], P(('tok', 'voc')), may hold values from -60 to 60
- student_head: bfloat16 [2560, 98304], P(None, ('tok', 'voc'))
- target_ids: int32 [256, 2], replicated, may hold values from 0 to 98303
Outputs:
- sample_objective: float32 [256, 2], replicated
- grad_hidden: bfloat16 [256, 2, 2560], P(('tok', 'voc'))
- grad_head: bfloat16 [2560, 98304], P(None, ('tok', 'voc'))
All inputs are finite; a program needn't handle non-finite values.
Results may differ from a plain program's by a relative error of at most 0.0044.
Values may be sent and summed in bfloat16 or wider, within the bound.
No kernel may reach another device: no remote copies, remote signals or barrier semaphores. Data moves between devices by JAX's collectives and lax.ppermute only.
A program may use at most 128 MiB of HBM per device.

v0:
```python
import jax
import jax.numpy as jnp
from jax import lax
from jax.sharding import PartitionSpec as P

smoothing_scale = 2.0
distill_coefficient = 0.5


def shift_rows(values, fill):
    return jnp.concatenate([values[1:], jnp.full_like(values[:1], fill)], axis=0)


def local(teacher_hidden, teacher_head, student_hidden, student_head, target_ids):
    tok_count = lax.axis_size("tok")
    voc_count = lax.axis_size("voc")
    stripes = teacher_head.shape[1]
    local_vocab = teacher_head.shape[2]
    flat_head = teacher_head.reshape(teacher_head.shape[0], stripes * local_vocab)
    all_rows = teacher_hidden.shape[0]
    feature_width = student_head.shape[0]
    gathered = lax.all_gather(student_hidden, ("tok", "voc"), axis=0, tiled=True)
    gathered_flat = gathered.reshape(all_rows * 2, feature_width)
    pupil_scores = jnp.dot(gathered_flat, student_head, preferred_element_type=jnp.float32).reshape(
        all_rows, 2, local_vocab
    )
    vocab_base = (lax.axis_index("tok") * voc_count + lax.axis_index("voc")) * local_vocab
    columns = lax.broadcasted_iota(jnp.int32, (1, 1, local_vocab), 2) + vocab_base
    matches = columns == target_ids[:, :, None]
    target_part = jnp.sum(jnp.where(matches, pupil_scores, 0.0), axis=2)
    pupil_scaled_scores = pupil_scores / smoothing_scale
    row_block = teacher_hidden
    teacher_tile = (
        lax.psum_scatter(
            jnp.dot(row_block, flat_head, preferred_element_type=jnp.float32),
            "tok",
            scatter_dimension=0,
            tiled=True,
        )
        / smoothing_scale
    )
    teacher_peak = lax.pmax(jnp.max(teacher_tile, axis=1), "voc")
    teacher_total = lax.psum(jnp.sum(jnp.exp(teacher_tile - teacher_peak[:, None]), axis=1), "voc")
    logprob = teacher_tile - (teacher_peak + jnp.log(teacher_total))[:, None]
    logprob = logprob.reshape(all_rows // tok_count, stripes, local_vocab)
    own_logprob = lax.all_to_all(logprob, "tok", split_axis=1, concat_axis=0, tiled=True).reshape(
        all_rows, local_vocab
    )
    correct_class_logscore = jnp.stack([own_logprob, shift_rows(own_logprob, 0.0)], axis=1)
    pupil_peak_score = lax.pmax(jnp.max(pupil_scores, axis=2), ("tok", "voc"))
    shifted_scores = pupil_scores - pupil_peak_score[:, :, None]
    exp_one = jnp.exp(shifted_scores)
    scaled_exponential = jnp.exp(shifted_scores / smoothing_scale)
    tutor_likelihood = jnp.exp(correct_class_logscore)
    sum_one, scaled_accumulation, mixed_expectation, target_logit = lax.psum(
        (
            jnp.sum(exp_one, axis=2),
            jnp.sum(scaled_exponential, axis=2),
            jnp.sum(tutor_likelihood * (correct_class_logscore - pupil_scaled_scores), axis=2),
            target_part,
        ),
        ("tok", "voc"),
    )
    lse_one = pupil_peak_score + jnp.log(sum_one)
    scaled_normalizer = pupil_peak_score / smoothing_scale + jnp.log(scaled_accumulation)
    row_index = lax.broadcasted_iota(jnp.int32, (all_rows, 2), 0)
    head_index = lax.broadcasted_iota(jnp.int32, (all_rows, 2), 1)
    sample_coefficient = jnp.where(
        (head_index == 1) & (row_index == all_rows - 1), 0.0, 1.0
    ).astype(jnp.float32)
    sample_objective = sample_coefficient * (
        distill_coefficient * smoothing_scale**2 * (mixed_expectation + scaled_normalizer)
        + (1.0 - distill_coefficient) * (lse_one - target_logit)
    )
    score_derivative = (
        sample_coefficient[:, :, None]
        * (
            distill_coefficient
            * smoothing_scale
            * (scaled_exponential / scaled_accumulation[:, :, None] - tutor_likelihood)
            + (1.0 - distill_coefficient)
            * (exp_one / sum_one[:, :, None] - matches.astype(jnp.float32))
        )
    ).astype(jnp.bfloat16)
    grad_flat = score_derivative.reshape(all_rows * 2, local_vocab)
    row_block = grad_flat
    product = lax.dot_general(
        row_block, student_head, (((1,), (1,)), ((), ())), preferred_element_type=jnp.float32
    )
    grad_hidden = lax.psum_scatter(
        product.reshape(
            all_rows // (tok_count * voc_count) * lax.axis_size(("tok", "voc")), 2, feature_width
        ),
        ("tok", "voc"),
        scatter_dimension=0,
        tiled=True,
    ).astype(jnp.bfloat16)
    grad_head = lax.dot_general(
        gathered_flat, grad_flat, (((0,), (0,)), ((), ())), preferred_element_type=jnp.float32
    ).astype(jnp.bfloat16)
    return (sample_objective, grad_hidden, grad_head)


def solution(mesh):
    return jax.shard_map(
        local,
        mesh=mesh,
        in_specs=(
            P(None, "tok"),
            P("tok", None, "voc"),
            P(("tok", "voc"), None, None),
            P(None, ("tok", "voc")),
            P(),
        ),
        out_specs=(P(), P(("tok", "voc"), None, None), P(None, ("tok", "voc"))),
        check_vma=False,
    )
```

profile of v0, /device:TPU:0, one launch (start us, length us, event | category | flops | bytes accessed | tf_op | source)
XLA Modules:
  0.0 453.4 jit_solution(7680793724077952243)
XLA Ops:
  8.0 0.0 copy-start
  8.0 0.0 reduce-scatter.3.cloned.1.call-start
  8.1 4.8 %copy.24 = bf16[64,8,8,768]{3,1,2,0:T(8,128)(2,1)S(1)} copy(bf16[64,8,8,768]{3,2,1,0:T(8,128)(2,1)} %bitcast.35) | data formatting | bytes 12582912
  12.9 0.0 copy-done
  12.9 4.5 fusion.17
  17.3 0.0 reduce-scatter.3.cloned.1.call-update
  17.4 0.0 all-gather.2.cloned.1.call-start
  17.4 0.5 all-gather.2.cloned.1.call-update
  18.0 0.1 and_select_fusion
  18.1 102.8 %reduce-scatter.3.cloned.1.call-done = f32[32,6144]{1,0:T(8,128)} async-done(((f32[256,6144]{1,0:T(8,128)}), f32[32,6144]{1,0:T(8,128)}) %reduce-scatter.3.cloned.1.call-update) | async-done | bytes 786448 | tf_op jit(solution)/shard_map/reduce_scatter | solution.py:34
  120.8 1.4 multiply_reduce_fusion.1
  122.2 28.9 %pmax.14 = f32[32]{0:T(128)S(1)} all-reduce(f32[32]{0:T(128)S(1)} %multiply_reduce_fusion.1), channel_id=1, replica_groups=mesh['tok'=8,'voc'=16] {'voc'}, use_global_device_ids=true, to_apply=%region_2.3 | all-reduce | flops 32 | bytes 256 | tf_op jit(solution)/shard_map/pmax | solution.py:42
  151.1 1.4 exponential_reduce_fusion.1
  152.5 27.1 %psum.35 = f32[32]{0:T(128)S(1)} all-reduce(f32[32]{0:T(128)S(1)} %exponential_reduce_fusion.1), channel_id=1, replica_groups=mesh['tok'=8,'voc'=16] {'voc'}, use_global_device_ids=true, to_apply=%region_4.5 | all-reduce | flops 32 | bytes 256 | tf_op jit(solution)/shard_map/psum | solution.py:43
  179.7 0.1 multiply_subtract_fusion
  179.8 0.9 copy.32
  180.7 4.2 all-to-all-start
  184.9 0.0 all-gather.2.cloned.1.call-done
  185.0 5.2 %fusion.16 = (f32[256,2]{0,1:T(2,128)S(1)}, f32[256,2,768]{2,0,1:T(8,128)S(1)}) fusion(bf16[2560,768]{1,0:T(8,128)(2,1)} %param.8, bf16[256,2,2560]{2,1,0:T(2,128)(2,1)} %all-gather.2.cloned.1.call-done), kind=kOutput, calls=%fused_computation.33 | convolution fusion | flops 2013658624 | bytes 8128512 | tf_op jit(solution)/shard_map/dot_general | solution.py:24
  190.2 65.1 %pmax.15 = f32[256,2]{0,1:T(2,128)S(1)} all-reduce(f32[256,2]{0,1:T(2,128)S(1)} %get-tuple-element.18), channel_id=1, replica_groups=mesh['tok'=8,'voc'=16] {'tok','voc'}, use_global_device_ids=true, to_apply=%region_8.9 | all-reduce | flops 512 | bytes 4096 | tf_op jit(solution)/shard_map/pmax | solution.py:50
  255.3 0.0 all-to-all-done
  255.3 0.1 slice.4
  255.4 0.1 pad_bitcast_fusion
  255.4 0.6 copy-done.2
  256.0 1.1 fusion.13
  257.1 64.6 %all-reduce.3 = (f32[256,2]{0,1:T(2,128)S(1)}, f32[256,2]{0,1:T(2,128)S(1)}) all-reduce(f32[256,2]{0,1:T(2,128)S(1)} %get-tuple-element.10, f32[256,2]{0,1:T(2,128)S(1)} %get-tuple-element.9), channel_id=1, replica_groups=mesh['tok'=8,'voc'=16] {'tok','voc'}, use_global_device_ids=true, to_apply=%region_12.13 | all-reduce | flops 1024 | bytes 8192 | tf_op jit(solution)/shard_map/psum | solution.py:55
  321.8 7.1 %fusion.1 = f32[256,2,2560]{2,0,1:T(8,128)} fusion(bf16[2560,768]{1,0:T(8,128)(2,1)} %param.8, f32[256,2,768]{2,0,1:T(8,128)S(1)} %get-tuple-element.19, f32[256,1,768]{2,0,1:T(8,128)S(1)} %pad_bitcast_fusion, f32[256,1,768]{2,0,1:T(8,128)S(1)} %bitcast.33, f32[256,2]{0,1:T(2,128)S(1)} %get-tuple-element.16, f32[256,2]{0,1:T(2,128)S(1)} %get-tuple-element.17, ...), kind=kOutput, calls=%fused_computation.2 | convolution fusion | flops 2018377728 | bytes 12334080 | tf_op jit(solution)/shard_map/dot_general | solution.py:87
  328.9 4.9 %fusion = bf16[2560,768]{0,1:T(8,128)(2,1)} fusion(bf16[256,2,2560]{2,1,0:T(2,128)(2,1)S(1)} %copy-done.3, f32[256,2,768]{2,0,1:T(8,128)S(1)} %get-tuple-element.19, f32[256,1,768]{2,0,1:T(8,128)S(1)} %pad_bitcast_fusion, f32[256,1,768]{2,0,1:T(8,128)S(1)} %bitcast.34, f32[256,2]{0,1:T(2,128)S(1)} %get-tuple-element.16, f32[256,2]{0,1:T(2,128)S(1)} %get-tuple-element.17, ...), kind=kOutput, calls=%fused_computation.1 | convolution fusion | flops 2020343808 | bytes 9712640 | tf_op jit(solution)/shard_map/dot_general | solution.py:98
  333.8 6.3 %copy.19 = bf16[2560,768]{1,0:T(8,128)(2,1)} copy(bf16[2560,768]{0,1:T(8,128)(2,1)} %fusion) | data formatting | bytes 7864320
  340.0 104.6 %all-reduce.5 = (f32[256,2]{0,1:T(2,128)S(1)}, f32[256,2]{0,1:T(2,128)S(1)}, bf16[256,2,2560]{2,0,1:T(8,128)(2,1)S(1)}) all-reduce(f32[256,2]{0,1:T(2,128)S(1)} %get-tuple-element.11, f32[256,2]{0,1:T(2,128)S(1)} %get-tuple-element.12, f32[256,2,2560]{2,0,1:T(8,128)} %fusion.1), channel_id=1, replica_groups=mesh['tok'=8,'voc'=16] {'tok','voc'}, use_global_device_ids=true, to_apply=%region_14.15 | all-reduce | flops 1311744 | bytes 7872512 | tf_op jit(solution)/shard_map/psum | solution.py:55
  444.7 0.6 copy.18
  445.4 0.6 add_multiply_fusion
  (10 shorter events, 0.1 us)
Async XLA Ops:
  8.0 4.9 %copy-start = (bf16[256,512]{1,0:T(8,128)(2,1)S(1)}, bf16[256,512]{1,0:T(8,128)(2,1)}, u32[]{:S(2)}) copy-start(bf16[256,512]{1,0:T(8,128)(2,1)} %param.5) | copy-start | bytes 786436
  8.0 112.8 %reduce-scatter.3.cloned.1.call-start = ((), (), s32[]{:S(2)}) async-start(), calls=%async_computation.2 | async-start | bytes 7077888 | tf_op jit(solution)/shard_map/reduce_scatter | solution.py:34
  17.4 167.6 %all-gather.2.cloned.1.call-start = ((), (), s32[]{:S(2)}) async-start(), calls=%async_computation.3 | async-start | bytes 2641920 | tf_op jit(solution)/shard_map/all_gather | solution.py:22
  120.8 58.8 %copy-start.1 = (f32[32,6144]{1,0:T(8,128)S(1)}, f32[32,6144]{1,0:T(8,128)}, u32[]{:S(2)}) copy-start(f32[32,6144]{1,0:T(8,128)} %reduce-scatter.3.cloned.1.call-done) | copy-start | bytes 2359300
  180.7 74.6 %all-to-all-start = ((f32[32,8,768]{2,0,1:T(8,128)}), f32[32,8,768]{2,0,1:T(8,128)S(1)}, u32[]{:S(2)}, u32[]{:S(2)}) async-start(f32[32,8,768]{2,0,1:T(8,128)} %bitcast.29), calls=%async_computation.1 | async-start | bytes 1572864 | tf_op jit(solution)/shard_map/all_to_all | solution.py:46
  255.3 0.7 copy-start.2
  321.8 7.1 %copy-start.3 = (bf16[256,2,2560]{2,1,0:T(2,128)(2,1)S(1)}, bf16[256,2,2560]{2,1,0:T(2,128)(2,1)}, u32[]{:S(2)}) copy-start(bf16[256,2,2560]{2,1,0:T(2,128)(2,1)} %all-gather.2.cloned.1.call-done) | copy-start | bytes 7864324
Sparse Core Ops, SparseCore 0:
  17.5 103.2 reduce-scatter.2
Sparse Core Ops, SparseCore 1:
  21.0 75.4 all-gather.1
where the time goes:
time: 454 us; the launch traced here: 453 us
  blocking collectives  290 us (64%)
  waiting for transfers between devices  103 us (23%)
  matrix products  21.7 us (5%)
  between operations  15.6 us (3%)
  local copies, waits for them, and re-layouts  13.4 us (3%)
  other arithmetic  4.8 us (1%)
    psum x2, blocking collectives, local(): lax.psum((jnp.sum(exp_one, axis=2), jnp.sum(scaled_exponential, axis=2),...  169 us
    reduce_scatter x1, waiting for transfers between devices, local(): lax.psum_scatter(jnp.dot(row_block, flat_head, preferred_element_type=jnp...  103 us
    pmax x1, blocking collectives, local(): pupil_peak_score = lax.pmax(jnp.max(pupil_scores, axis=2), ('tok', 'voc'))  65.1 us
    pmax x1, blocking collectives, local(): teacher_peak = lax.pmax(jnp.max(teacher_tile, axis=1), 'voc')  28.9 us
    psum x1, blocking collectives, local(): lax.psum(jnp.sum(jnp.exp(teacher_tile - teacher_peak[:, None]), axis=1),...  27.1 us
    unnamed x11, local copies, waits for them, and re-layouts  12.3 us
  transfers between devices with their start and end apart: 3, of which 1 were waited for; matrix products, arithmetic and copies ran while one was open for 2% of the time, Pallas kernels for 0%

commit v1 on v0

v1 whole, which is shorter than its diff:
```python
import jax
import jax.numpy as jnp
from jax import lax
from jax.sharding import Mesh
from jax.sharding import PartitionSpec as P

TOK = ("x", "yh")
VOC = ("yl", "z", "c")
CHIPS = ("x", "yh", "yl", "z")
SIZES = (4, 2, 2, 4, 2)


def encode(partial):
    stripes, rows, width = partial.shape
    half = width // 2
    peak = jnp.maximum(jnp.max(jnp.abs(partial), axis=2), 1e-30)
    level = jnp.ceil(jnp.log2(peak) * 256.0)
    scale = jnp.exp2(-level / 256.0) * 32766.0
    code = jnp.clip(jnp.round(partial * scale[:, :, None]), -32767.0, 32767.0).astype(jnp.int32)
    words = (code[:, :, :half] << 16) | (code[:, :, half:] & 0xFFFF)
    tail = jnp.zeros((stripes, 8, half), jnp.int32).at[:, 0, :rows].set(level.astype(jnp.int32))
    return jnp.concatenate([words, tail], axis=1)


def decode(words, rows):
    level = words[:, rows, :rows].astype(jnp.float32)
    scale = (jnp.exp2(level / 256.0) * (0.5 / 32766.0))[:, :, None]
    body = words[:, :rows]
    high = (body >> 16).astype(jnp.float32)
    low = ((body << 16) >> 16).astype(jnp.float32)
    return jnp.concatenate([jnp.sum(high * scale, axis=0), jnp.sum(low * scale, axis=0)], axis=1)


def merge(parts):
    tp, tz, sp, s1, s2, cross, target = [parts[:, i] for i in range(7)]
    tm = jnp.max(tp, axis=0)
    sm = jnp.max(sp, axis=0)
    te = jnp.exp(tp - tm)
    se = jnp.exp((sp - sm) * 0.5)
    return jnp.stack(
        [
            tm,
            jnp.sum(tz * te, axis=0),
            sm,
            jnp.sum(s1 * (se * se), axis=0),
            jnp.sum(s2 * se, axis=0),
            jnp.sum(cross * te, axis=0),
            jnp.sum(target, axis=0),
        ]
    )


def everywhere(value, axes, count):
    copies = jnp.broadcast_to(value, (count,) + value.shape)
    return lax.all_to_all(copies, axes, 0, 0, tiled=True)


def local(teacher_hidden, teacher_head, student_hidden, student_head, target_ids):
    core = lax.axis_index("c")
    chips = lax.axis_size(CHIPS)
    stripes = teacher_head.shape[1]
    voc = teacher_head.shape[2]
    rows = teacher_hidden.shape[0]
    width = student_head.shape[0]
    base = lax.axis_index(TOK + VOC) * voc
    pair = [(0, 1), (1, 0)]

    partial = jnp.einsum("rd,dsv->srv", teacher_hidden, teacher_head, preferred_element_type=jnp.float32)
    words = lax.all_to_all(encode(partial), TOK, 0, 0, tiled=True)

    mine = jnp.swapaxes(student_hidden, 0, 1).reshape(4, width)
    own = everywhere(mine, CHIPS, chips).reshape(rows, width)
    other = lax.ppermute(own, "c", pair)
    hidden = jnp.concatenate([own, other], axis=0)
    scores = jnp.dot(hidden, student_head, preferred_element_type=jnp.float32)

    place = lax.broadcasted_iota(jnp.int32, (2 * rows, 1), 0)
    side = place // rows
    place = place % rows
    chip, head, inner = place // 4, (place // 2) % 2, place % 2
    row = chip * 4 + jnp.where(side == 0, core, 1 - core) * 2 + inner
    weight = jnp.where((head == 1) & (row == rows - 1), 0.0, 1.0).astype(jnp.float32)
    teacher_row = jnp.minimum(row + head, rows - 1)
    order = target_ids.reshape(chips, 2, 2, 2)
    order = jnp.transpose(order, (1, 0, 3, 2)).reshape(2, rows)
    ids = jnp.where(core == 0, order, order[::-1]).reshape(2 * rows, 1)
    match = lax.broadcasted_iota(jnp.int32, (1, voc), 1) + base == ids

    pick = (lax.broadcasted_iota(jnp.int32, (1, rows), 1) == teacher_row).astype(jnp.float32)
    teacher = jnp.dot(pick, decode(words, rows), precision=lax.Precision.HIGHEST)

    t_peak = jnp.max(teacher, axis=1, keepdims=True)
    t_exp = jnp.exp(teacher - t_peak)
    s_peak = jnp.max(scores, axis=1, keepdims=True)
    s_exp = jnp.exp((scores - s_peak) * 0.5)
    stats = jnp.stack(
        [
            t_peak[:, 0],
            jnp.sum(t_exp, axis=1),
            s_peak[:, 0],
            jnp.sum(s_exp * s_exp, axis=1),
            jnp.sum(s_exp, axis=1),
            jnp.sum(t_exp * (teacher - scores * 0.5), axis=1),
            jnp.sum(jnp.where(match, scores, 0.0), axis=1),
        ]
    )
    stats = jnp.where(core == 0, stats, jnp.roll(stats, rows, axis=1))
    stats = merge(everywhere(stats, VOC, lax.axis_size(VOC)))
    stats = merge(everywhere(stats, TOK, lax.axis_size(TOK)))
    tm, tz, sm, s1, s2, cross, target = [stats[i] for i in range(7)]
    t_lse = tm + jnp.log(tz)
    s_one = sm + jnp.log(s1)
    s_tau = sm * 0.5 + jnp.log(s2)
    objective = 2.0 * (cross / tz - t_lse + s_tau) + 0.5 * (s_one - target)
    objective = jnp.transpose(objective.reshape(2, chips, 2, 2), (1, 0, 3, 2)).reshape(rows, 2)
    last = (lax.broadcasted_iota(jnp.int32, (rows, 2), 0) == rows - 1) & (
        lax.broadcasted_iota(jnp.int32, (rows, 2), 1) == 1
    )
    objective = jnp.where(last, 0.0, objective)

    norms = jnp.stack([t_lse, s_one, s_tau])
    norms = jnp.where(core == 0, norms, jnp.roll(norms, rows, axis=1))[:, :, None]
    grad = weight * (
        jnp.exp(scores * 0.5 - norms[2])
        - jnp.exp(teacher - norms[0])
        + 0.5 * (jnp.exp(scores - norms[1]) - match.astype(jnp.float32))
    )
    grad = grad.astype(jnp.bfloat16)

    contract = (((1,), (1,)), ((), ()))
    give = lax.dot_general(grad[rows:], student_head, contract, preferred_element_type=jnp.float32)
    taken = lax.ppermute(give, "c", pair)
    keep = lax.dot_general(grad[:rows], student_head, contract, preferred_element_type=jnp.float32)
    grad_head = lax.dot_general(
        hidden, grad, (((0,), (0,)), ((), ())), preferred_element_type=jnp.float32
    ).astype(jnp.bfloat16)
    share = (keep + taken).astype(jnp.bfloat16).reshape(chips, 4, width)
    share = lax.all_to_all(share, CHIPS, 0, 0, tiled=True)
    grad_hidden = jnp.sum(share.astype(jnp.float32), axis=0).astype(jnp.bfloat16)
    grad_hidden = jnp.swapaxes(grad_hidden.reshape(2, 2, width), 0, 1)
    return objective, grad_hidden, grad_head


def solution(mesh):
    fine = Mesh(mesh.devices.reshape(SIZES), CHIPS + ("c",))
    return jax.shard_map(
        local,
        mesh=fine,
        in_specs=(
            P(None, TOK),
            P(TOK, None, VOC),
            P(TOK + VOC, None, None),
            P(None, TOK + VOC),
            P(),
        ),
        out_specs=(P(), P(TOK + VOC, None, None), P(None, TOK + VOC)),
        check_vma=False,
    )
```

time: 454 us -> 152 us (0.33)
  blocking collectives: 290 us -> 11.3 us
  waiting for transfers between devices: 103 us -> 69.9 us
  starting transfers between devices: 4.28 us -> 23.5 us
  between operations: 15.6 us -> 1.01 us
  local copies, waits for them, and re-layouts: 13.4 us -> 18.7 us
    psum x3 -> x0, blocking collectives: 196 us -> none  [the longest x2 169 us: local(): lax.psum((jnp.sum(exp_one, axis=2), jnp.sum(scaled_exponential, axis=2),...]
    reduce_scatter x1 -> x0, waiting for transfers between devices: 103 us -> none  [local(): lax.psum_scatter(jnp.dot(row_block, flat_head, preferred_element_type=jnp...]
    pmax x2 -> x0, blocking collectives: 94 us -> none  [the longest x1 65.1 us: local(): pupil_peak_score = lax.pmax(jnp.max(pupil_scores, axis=2), ('tok', 'voc'))]
    all_to_all x1 -> x4, waiting for transfers between devices: 0.01 us -> 65 us  [the longest x1 29.7 us: local(): words = lax.all_to_all(encode(partial), TOK, 0, 0, tiled=True)]
    all_to_all x1 -> x4, starting transfers between devices: 4.2 us -> 23.4 us  [the longest x2 15.1 us: everywhere(): return lax.all_to_all(copies, axes, 0, 0, tiled=True)]
    all_to_all x0 -> x1, blocking collectives: none -> 11.3 us  [everywhere(): return lax.all_to_all(copies, axes, 0, 0, tiled=True)]
    unnamed x11 -> x23, local copies, waits for them, and re-layouts: 12.3 us -> 5.49 us
    reshape x1 -> x7, local copies, waits for them, and re-layouts: 0.94 us -> 6.81 us  [the longest x1 3.39 us: local(): own = everywhere(mine, CHIPS, chips).reshape(rows, width)]
  transfers between devices with their start and end apart: 3 -> 6, of which waited for: 1 -> 5; matrix products, arithmetic and copies ran while one was open for 2% -> 19% of each run, Pallas kernels for 0% -> 0%
where the time goes in v1:
time: 152 us; the launch traced here: 151 us
  waiting for transfers between devices  69.9 us (46%)
  starting transfers between devices  23.5 us (15%)
  local copies, waits for them, and re-layouts  18.7 us (12%)
  matrix products  18.3 us (12%)
  blocking collectives  11.3 us (7%)
  other arithmetic  8.34 us (5%)
    all_to_all x1, waiting for transfers between devices, local(): words = lax.all_to_all(encode(partial), TOK, 0, 0, tiled=True)  29.7 us
    all_to_all x2, waiting for transfers between devices, everywhere(): return lax.all_to_all(copies, axes, 0, 0, tiled=True)  20.3 us
    all_to_all x2, starting transfers between devices, everywhere(): return lax.all_to_all(copies, axes, 0, 0, tiled=True)  15.1 us
    all_to_all x1, waiting for transfers between devices, local(): share = lax.all_to_all(share, CHIPS, 0, 0, tiled=True)  14.9 us
    all_to_all x1, blocking collectives, everywhere(): return lax.all_to_all(copies, axes, 0, 0, tiled=True)  11.3 us
    dot_general x1, matrix products, local(): lax.dot_general(hidden, grad, (((0,), (0,)), ((), ())), preferred_element...  5.91 us
    dot_general x1, matrix products, local(): jnp.einsum('rd,dsv->srv', teacher_hidden, teacher_head, preferred_element...  5.7 us
    unnamed x23, local copies, waits for them, and re-layouts  5.49 us
  transfers between devices with their start and end apart: 6, of which 5 were waited for; matrix products, arithmetic and copies ran while one was open for 19% of the time, Pallas kernels for 0%

profile of v1, /device:TPU:0, one launch (start us, length us, event | category | flops | bytes accessed | tf_op | source)
XLA Modules:
  0.0 151.1 jit_solution(11216162171612763796)
XLA Ops:
  0.6 0.8 copy.70
  1.5 1.4 broadcast_in_dim.46
  2.9 11.5 %all-to-all-start.1 = ((bf16[64,4,2560]{2,1,0:T(4,128)(2,1)}), bf16[64,4,2560]{2,1,0:T(4,128)(2,1)S(1)}, u32[]{:S(2)}, u32[]{:S(2)}) async-start(bf16[64,4,2560]{2,1,0:T(4,128)(2,1)} %broadcast_in_dim.46), calls=%async_computation.1 | async-start | bytes 2621440 | tf_op jit(solution)/shard_map/all_to_all | solution.py:55
  14.4 5.7 %abs_reduce_fusion = (f32[8,256]{1,0:T(8,128)S(1)}, f32[8,768,256]{1,2,0:T(8,128)S(1)}) fusion(bf16[512,8,768]{2,1,0:T(8,128)(2,1)} %param.8, bf16[256,512]{1,0:T(8,128)(2,1)S(1)} %copy-done), kind=kOutput, calls=%fused_computation.3 | convolution fusion | flops 1613756416 | bytes 12853248 | tf_op jit(solution)/shard_map/rd,dsv->srv/dot_general | solution.py:68
  20.1 0.8 convert_bitcast_fusion
  21.2 1.9 %pad_add_fusion = s32[8,264,384]{2,1,0:T(8,128)} fusion(s32[8,1,256]{2,1,0:T(1,128)S(1)} %reshape.380, s32[8,256,384]{2,1,0:T(8,128)S(1)} %fusion.3), kind=kLoop, calls=%fused_computation.7 | loop fusion | flops 811008 | bytes 6397952 | tf_op jit(solution)/shard_map/concatenate | solution.py:22
  23.1 12.7 %all-to-all-done.1 = bf16[64,4,2560]{2,1,0:T(4,128)(2,1)S(1)} async-done(((bf16[64,4,2560]{2,1,0:T(4,128)(2,1)}), bf16[64,4,2560]{2,1,0:T(4,128)(2,1)S(1)}, u32[]{:S(2)}, u32[]{:S(2)}) %all-to-all-start.1) | async-done | bytes 1310752 | tf_op jit(solution)/shard_map/all_to_all | solution.py:55
  35.8 1.1 copy-done.5
  36.9 3.7 %all-to-all-start = ((s32[8,264,384]{2,1,0:T(8,128)}), s32[8,264,384]{2,1,0:T(8,128)S(1)}, u32[]{:S(2)}, u32[]{:S(2)}) async-start(s32[8,264,384]{2,1,0:T(8,128)} %pad_add_fusion), calls=%async_computation | async-start | bytes 6488064 | tf_op jit(solution)/shard_map/all_to_all | solution.py:69
  40.6 3.4 %reshape.374 = bf16[256,2560]{1,0:T(8,128)(2,1)} reshape(bf16[64,4,2560]{2,1,0:T(4,128)(2,1)} %copy-done.5) | data formatting | bytes 2621440 | tf_op jit(solution)/shard_map/reshape | solution.py:72
  44.0 0.9 reshape.375
  44.8 1.7 %copy.71 = s32[2,64,2,2]{3,2,1,0:T(2,128)} copy(s32[2,64,2,2]{3,0,1,2:T(2,128)} %bitcast.131) | data formatting | bytes 4096 | tf_op jit(solution)/shard_map/transpose | solution.py:85
  46.5 1.1 reshape.376
  47.8 1.6 %constant_dynamic-update-slice_fusion.1 = bf16[512,2560]{1,0:T(8,128)(2,1)S(1)} fusion(bf16[256,2560]{1,0:T(8,128)(2,1)} %reshape.374), kind=kLoop, calls=%fused_computation.85 | loop fusion | bytes 2621440
  49.3 1.4 constant_dynamic-update-slice_fusion
  50.8 1.5 copy-done.8
  52.3 3.3 %fusion.68 = (f32[512]{0:T(512)S(1)}, f32[512,768]{1,0:T(8,128)}) fusion(bf16[512,2560]{1,0:T(8,128)(2,1)S(1)} %constant_dynamic-update-slice_fusion, bf16[2560,768]{1,0:T(8,128)(2,1)S(1)} %copy-done.1), kind=kOutput, calls=%fused_computation.138 | convolution fusion | flops 2013658624 | bytes 8128512 | tf_op jit(solution)/shard_map/dot_general | solution.py:75
  55.6 29.7 %all-to-all-done = s32[8,264,384]{2,1,0:T(8,128)S(1)} async-done(((s32[8,264,384]{2,1,0:T(8,128)}), s32[8,264,384]{2,1,0:T(8,128)S(1)}, u32[]{:S(2)}, u32[]{:S(2)}) %all-to-all-start) | async-done | bytes 3244064 | tf_op jit(solution)/shard_map/all_to_all | solution.py:69
  85.3 0.9 multiply_reduce_fusion.1
  86.3 1.0 fusion.67
  87.3 1.5 multiply_reduce_fusion.2
  88.9 11.3 %all_to_all.25 = f32[16,7,512]{2,1,0:T(8,128)S(1)} all-to-all(f32[16,7,512]{2,1,0:T(8,128)S(1)} %broadcast_in_dim.48), channel_id=1, replica_groups=mesh['x'=4,'yh'=2,'yl'=2,'z'=4,'c'=2] {'yl','z','c'}, dimensions={0} | all-to-all | bytes 458752 | tf_op jit(solution)/shard_map/all_to_all | solution.py:55
  101.2 3.6 %all-to-all-start.3 = ((f32[8,7,512]{2,1,0:T(8,128)}), f32[8,7,512]{2,1,0:T(8,128)S(1)}, u32[]{:S(2)}, u32[]{:S(2)}) async-start(f32[8,7,512]{2,1,0:T(8,128)} %broadcast_in_dim.49), calls=%async_computation.3 | async-start | bytes 262144 | tf_op jit(solution)/shard_map/all_to_all | solution.py:55
  104.7 7.6 %all-to-all-done.3 = f32[8,7,512]{2,1,0:T(8,128)S(1)} async-done(((f32[8,7,512]{2,1,0:T(8,128)}), f32[8,7,512]{2,1,0:T(8,128)S(1)}, u32[]{:S(2)}, u32[]{:S(2)}) %all-to-all-start.3) | async-done | bytes 114720 | tf_op jit(solution)/shard_map/all_to_all | solution.py:55
  112.7 1.1 fusion.9
  114.5 1.2 fusion.16
  115.8 4.9 %collective-permute-done.1 = f32[256,2560]{1,0:T(8,128)S(1)} collective-permute-done((f32[256,2560]{1,0:T(8,128)S(1)}, f32[256,2560]{1,0:T(8,128)S(1)}, u32[]{:S(2)}, u32[]{:S(2)}) %collective-permute-start.1) | collective-permute-done | bytes 2621472 | tf_op jit(solution)/shard_map/ppermute | solution.py:132
  120.7 1.2 fusion.2
  121.9 1.3 reshape.378
  123.2 4.7 %all-to-all-start.4 = ((bf16[64,4,2560]{2,1,0:T(4,128)(2,1)}), bf16[64,4,2560]{2,1,0:T(4,128)(2,1)S(1)}, u32[]{:S(2)}, u32[]{:S(2)}) async-start(bf16[64,4,2560]{2,1,0:T(4,128)(2,1)} %reshape.378), calls=%async_computation.4 | async-start | bytes 2621440 | tf_op jit(solution)/shard_map/all_to_all | solution.py:138
  129.1 5.9 %convolution_convert_fusion = bf16[2560,768]{1,0:T(8,128)(2,1)} fusion(bf16[512,2560]{1,0:T(8,128)(2,1)} %copy-done.8, bf16[512,768]{1,0:T(8,128)(2,1)S(1)} %copy-done.7), kind=kOutput, calls=%fused_computation.4 | convolution fusion | flops 2015232000 | bytes 7340032 | tf_op jit(solution)/shard_map/dot_general | solution.py:134
  135.0 14.9 %all-to-all-done.4 = bf16[64,4,2560]{2,1,0:T(4,128)(2,1)S(1)} async-done(((bf16[64,4,2560]{2,1,0:T(4,128)(2,1)}), bf16[64,4,2560]{2,1,0:T(4,128)(2,1)S(1)}, u32[]{:S(2)}, u32[]{:S(2)}) %all-to-all-start.4) | async-done | bytes 1310752 | tf_op jit(solution)/shard_map/all_to_all | solution.py:138
  (58 shorter events, 4.9 us)
Async XLA Ops:
  0.6 13.7 %copy-start = (bf16[256,512]{1,0:T(8,128)(2,1)S(1)}, bf16[256,512]{1,0:T(8,128)(2,1)}, u32[]{:S(2)}) copy-start(bf16[256,512]{1,0:T(8,128)(2,1)} %param.7) | copy-start | bytes 786436
  2.9 33.0 %all-to-all-start.1 = ((bf16[64,4,2560]{2,1,0:T(4,128)(2,1)}), bf16[64,4,2560]{2,1,0:T(4,128)(2,1)S(1)}, u32[]{:S(2)}, u32[]{:S(2)}) async-start(bf16[64,4,2560]{2,1,0:T(4,128)(2,1)} %broadcast_in_dim.46), calls=%async_computation.1 | async-start | bytes 2621440 | tf_op jit(solution)/shard_map/all_to_all | solution.py:55
  35.8 1.1 copy-start.5
  36.9 48.4 %all-to-all-start = ((s32[8,264,384]{2,1,0:T(8,128)}), s32[8,264,384]{2,1,0:T(8,128)S(1)}, u32[]{:S(2)}, u32[]{:S(2)}) async-start(s32[8,264,384]{2,1,0:T(8,128)} %pad_add_fusion), calls=%async_computation | async-start | bytes 6488064 | tf_op jit(solution)/shard_map/all_to_all | solution.py:69
  40.6 3.4 %copy-start.9 = (s32[256,2]{0,1:T(2,128)S(1)}, s32[256,2]{0,1:T(2,128)}, u32[]{:S(2)}) copy-start(s32[256,2]{0,1:T(2,128)} %param.11) | copy-start | bytes 6148
  44.0 5.4 %collective-permute-start = (bf16[256,2560]{1,0:T(8,128)(2,1)}, bf16[256,2560]{1,0:T(8,128)(2,1)}, u32[]{:S(2)}, u32[]{:S(2)}) collective-permute-start(bf16[256,2560]{1,0:T(8,128)(2,1)} %reshape.374), channel_id=1, source_target_pairs={{0,1},{1,0},{2,3},{3,2},{4,5},{5,4},{6,7},{7,6},{8,9},{9,8},{10,11... | collective-permute-start | bytes 3932168 | tf_op jit(solution)/shard_map/ppermute | solution.py:73
  47.8 4.5 %copy-start.1 = (bf16[2560,768]{1,0:T(8,128)(2,1)S(1)}, bf16[2560,768]{1,0:T(8,128)(2,1)}, u32[]{:S(2)}) copy-start(bf16[2560,768]{1,0:T(8,128)(2,1)} %param.10) | copy-start | bytes 11796484
  50.7 1.5 copy-start.8
  85.3 1.9 %copy-start.3 = (f32[512,768]{1,0:T(8,128)S(1)}, f32[512,768]{1,0:T(8,128)}, u32[]{:S(2)}) copy-start(f32[512,768]{1,0:T(8,128)} %get-tuple-element.90) | copy-start | bytes 4718596
  87.3 25.4 %copy-start.4 = (f32[512,768]{1,0:T(8,128)S(1)}, f32[512,768]{1,0:T(8,128)}, u32[]{:S(2)}) copy-start(f32[512,768]{1,0:T(8,128)} %get-tuple-element.90) | copy-start | bytes 4718596
  101.2 11.2 %all-to-all-start.3 = ((f32[8,7,512]{2,1,0:T(8,128)}), f32[8,7,512]{2,1,0:T(8,128)S(1)}, u32[]{:S(2)}, u32[]{:S(2)}) async-start(f32[8,7,512]{2,1,0:T(8,128)} %broadcast_in_dim.49), calls=%async_computation.3 | async-start | bytes 262144 | tf_op jit(solution)/shard_map/all_to_all | solution.py:55
  112.4 2.1 %copy-start.2 = (bf16[2560,768]{1,0:T(8,128)(2,1)S(1)}, bf16[2560,768]{1,0:T(8,128)(2,1)}, u32[]{:S(2)}) copy-start(bf16[2560,768]{1,0:T(8,128)(2,1)} %param.10) | copy-start | bytes 11796484
  114.5 6.2 %copy-start.6 = (bf16[512,768]{1,0:T(8,128)(2,1)}, bf16[512,768]{1,0:T(8,128)(2,1)S(1)}, u32[]{:S(2)}) copy-start(bf16[512,768]{1,0:T(8,128)(2,1)S(1)} %fusion.9) | copy-start | bytes 2359300
  115.7 5.0 %collective-permute-start.1 = (f32[256,2560]{1,0:T(8,128)S(1)}, f32[256,2560]{1,0:T(8,128)S(1)}, u32[]{:S(2)}, u32[]{:S(2)}) collective-permute-start(f32[256,2560]{1,0:T(8,128)S(1)} %fusion.16), channel_id=1, source_target_pairs={{0,1},{1,0},{2,3},{3,2},{4,5},{5,4},{6,7},{7,6},{8,9},{9,8},{10,11... | collective-permute-start | bytes 7864328 | tf_op jit(solution)/shard_map/ppermute | solution.py:132
  121.9 7.1 %copy-start.7 = (bf16[512,768]{1,0:T(8,128)(2,1)S(1)}, bf16[512,768]{1,0:T(8,128)(2,1)}, u32[]{:S(2)}) copy-start(bf16[512,768]{1,0:T(8,128)(2,1)} %copy-done.6) | copy-start | bytes 2359300
  123.2 26.7 %all-to-all-start.4 = ((bf16[64,4,2560]{2,1,0:T(4,128)(2,1)}), bf16[64,4,2560]{2,1,0:T(4,128)(2,1)S(1)}, u32[]{:S(2)}, u32[]{:S(2)}) async-start(bf16[64,4,2560]{2,1,0:T(4,128)(2,1)} %reshape.378), calls=%async_computation.4 | async-start | bytes 2621440 | tf_op jit(solution)/shard_map/all_to_all | solution.py:138

commit v2 on v1

--- a/solution.py
+++ b/solution.py
@@ -8,6 +8,7 @@
 VOC = ("yl", "z", "c")
 CHIPS = ("x", "yh", "yl", "z")
 SIZES = (4, 2, 2, 4, 2)
+WALK = ("z", "yh", "yl", "x")
 
 
 def encode(partial):
@@ -50,6 +51,17 @@
     )
 
 
+def ring_gather(block, axes):
+    size = lax.axis_size(axes)
+    here = lax.axis_index(axes)
+    whole = jnp.zeros((size,) + block.shape, block.dtype)
+    whole = lax.dynamic_update_index_in_dim(whole, block, here, 0)
+    for step in range(1, size):
+        taken = lax.ppermute(block, axes, [(i, (i + step) % size) for i in range(size)])
+        whole = lax.dynamic_update_index_in_dim(whole, taken, (here + size - step) % size, 0)
+    return whole.reshape((size * block.shape[0],) + block.shape[1:])
+
+
 def everywhere(value, axes, count):
     copies = jnp.broadcast_to(value, (count,) + value.shape)
     return lax.all_to_all(copies, axes, 0, 0, tiled=True)
@@ -68,8 +80,9 @@
     partial = jnp.einsum("rd,dsv->srv", teacher_hidden, teacher_head, preferred_element_type=jnp.float32)
     words = lax.all_to_all(encode(partial), TOK, 0, 0, tiled=True)
 
-    mine = jnp.swapaxes(student_hidden, 0, 1).reshape(4, width)
-    own = everywhere(mine, CHIPS, chips).reshape(rows, width)
+    own = jnp.swapaxes(student_hidden, 0, 1).reshape(4, width)
+    for axes in ("x", ("yh", "yl"), "z"):
+        own = ring_gather(own, axes)
     other = lax.ppermute(own, "c", pair)
     hidden = jnp.concatenate([own, other], axis=0)
     scores = jnp.dot(hidden, student_head, preferred_element_type=jnp.float32)
@@ -77,12 +90,13 @@
     place = lax.broadcasted_iota(jnp.int32, (2 * rows, 1), 0)
     side = place // rows
     place = place % rows
-    chip, head, inner = place // 4, (place // 2) % 2, place % 2
+    head, inner = (place // 2) % 2, place % 2
+    chip = (place // 4) % 4 * 16 + (place // 16) % 4 * 4 + place // 64
     row = chip * 4 + jnp.where(side == 0, core, 1 - core) * 2 + inner
     weight = jnp.where((head == 1) & (row == rows - 1), 0.0, 1.0).astype(jnp.float32)
     teacher_row = jnp.minimum(row + head, rows - 1)
-    order = target_ids.reshape(chips, 2, 2, 2)
-    order = jnp.transpose(order, (1, 0, 3, 2)).reshape(2, rows)
+    order = target_ids.reshape(4, 4, 4, 2, 2, 2)
+    order = jnp.transpose(order, (3, 2, 1, 0, 5, 4)).reshape(2, rows)
     ids = jnp.where(core == 0, order, order[::-1]).reshape(2 * rows, 1)
     match = lax.broadcasted_iota(jnp.int32, (1, voc), 1) + base == ids
 
@@ -112,7 +126,8 @@
     s_one = sm + jnp.log(s1)
     s_tau = sm * 0.5 + jnp.log(s2)
     objective = 2.0 * (cross / tz - t_lse + s_tau) + 0.5 * (s_one - target)
-    objective = jnp.transpose(objective.reshape(2, chips, 2, 2), (1, 0, 3, 2)).reshape(rows, 2)
+    objective = objective.reshape(2, 4, 4, 4, 2, 2)
+    objective = jnp.transpose(objective, (3, 2, 1, 0, 5, 4)).reshape(rows, 2)
     last = (lax.broadcasted_iota(jnp.int32, (rows, 2), 0) == rows - 1) & (
         lax.broadcasted_iota(jnp.int32, (rows, 2), 1) == 1
     )
@@ -135,7 +150,7 @@
         hidden, grad, (((0,), (0,)), ((), ())), preferred_element_type=jnp.float32
     ).astype(jnp.bfloat16)
     share = (keep + taken).astype(jnp.bfloat16).reshape(chips, 4, width)
-    share = lax.all_to_all(share, CHIPS, 0, 0, tiled=True)
+    share = lax.all_to_all(share, WALK, 0, 0, tiled=True)
     grad_hidden = jnp.sum(share.astype(jnp.float32), axis=0).astype(jnp.bfloat16)
     grad_hidden = jnp.swapaxes(grad_hidden.reshape(2, 2, width), 0, 1)
     return objective, grad_hidden, grad_head

time: 152 us -> 162 us (1.066)
  starting transfers between devices: 23.5 us -> 32.8 us
  waiting for transfers between devices: 69.9 us -> 63.6 us
  local copies, waits for them, and re-layouts: 18.7 us -> 22.5 us
  matrix products: 18.3 us -> 21.2 us
    ppermute x0 -> x9, waiting for transfers between devices: none -> 35.9 us  [ring_gather(): lax.ppermute(block, axes, [(i, (i + step) % size) for i in range(size)])]
    all_to_all x1, waiting for transfers between devices: 29.7 us -> 0.01 us  [local(): words = lax.all_to_all(encode(partial), TOK, 0, 0, tiled=True)]
    ppermute x0 -> x9, starting transfers between devices: none -> 18.5 us  [ring_gather(): lax.ppermute(block, axes, [(i, (i + step) % size) for i in range(size)])]
    all_to_all x2 -> x1, waiting for transfers between devices: 20.3 us -> 7.89 us  [everywhere(): return lax.all_to_all(copies, axes, 0, 0, tiled=True)]
    all_to_all x2 -> x1, starting transfers between devices: 15.1 us -> 4.85 us  [everywhere(): return lax.all_to_all(copies, axes, 0, 0, tiled=True)]
    dynamic_update_slice x0 -> x12, local copies, waits for them, and re-layouts: none -> 8.6 us  [the longest x9 6.32 us: ring_gather(): lax.dynamic_update_index_in_dim(whole, taken, (here + size - step) % size...]
    unnamed x23 -> x16, local copies, waits for them, and re-layouts: 5.49 us -> 1.35 us
    broadcast_in_dim x0 -> x5, local copies, waits for them, and re-layouts: none -> 3.39 us  [the longest x3 1.83 us: ring_gather(): whole = jnp.zeros((size,) + block.shape, block.dtype)]
  transfers between devices with their start and end apart: 6 -> 14, of which waited for: 5 -> 7; matrix products, arithmetic and copies ran while one was open for 19% -> 24% of each run, Pallas kernels for 0% -> 0%
where the time goes in v2:
time: 162 us
  waiting for transfers between devices  63.6 us (39%)
  starting transfers between devices  32.8 us (20%)
  local copies, waits for them, and re-layouts  22.5 us (14%)
  matrix products  21.2 us (13%)
  blocking collectives  12 us (7%)
  other arithmetic  8.35 us (5%)
    ppermute x9, waiting for transfers between devices, ring_gather(): lax.ppermute(block, axes, [(i, (i + step) % size) for i in range(size)])  35.9 us
    ppermute x9, starting transfers between devices, ring_gather(): lax.ppermute(block, axes, [(i, (i + step) % size) for i in range(size)])  18.5 us
    all_to_all x1, waiting for transfers between devices, local(): share = lax.all_to_all(share, WALK, 0, 0, tiled=True)  14.9 us
    all_to_all x1, blocking collectives, everywhere(): return lax.all_to_all(copies, axes, 0, 0, tiled=True)  12 us
    all_to_all x1, waiting for transfers between devices, everywhere(): return lax.all_to_all(copies, axes, 0, 0, tiled=True)  7.89 us
    dynamic_update_slice x9, local copies, waits for them, and re-layouts, ring_gather(): lax.dynamic_update_index_in_dim(whole, taken, (here + size - step) % size...  6.32 us
    dot_general x1, matrix products, local(): scores = jnp.dot(hidden, student_head, preferred_element_type=jnp.float32)  6.27 us
    dot_general x1, matrix products, local(): lax.dot_general(hidden, grad, (((0,), (0,)), ((), ())), preferred_element...  5.88 us
  transfers between devices with their start and end apart: 14, of which 7 were waited for; matrix products, arithmetic and copies ran while one was open for 24% of the time, Pallas kernels for 0%

profile of v2, /device:TPU:0, one launch (start us, length us, event | category | flops | bytes accessed | tf_op | source)
XLA Modules:
  0.0 161.5 jit_solution(13486224006325417921)
XLA Ops:
  2.1 1.6 collective-permute-start
  3.6 2.7 %collective-permute-start.1 = (bf16[4,2560]{1,0:T(4,128)(2,1)}, bf16[4,2560]{1,0:T(4,128)(2,1)}, u32[]{:S(2)}, u32[]{:S(2)}) collective-permute-start(bf16[4,2560]{1,0:T(4,128)(2,1)} %reshape.478), channel_id=1, source_target_pairs={{0,64},{32,96},{64,0},{96,32},{1,65},{33,97},{65,1},{97,33},{2,66}... | collective-permute-start | bytes 61448 | tf_op jit(solution)/shard_map/ppermute | solution.py:60
  6.4 1.4 collective-permute-start.2
  7.8 5.7 %abs_reduce_fusion = (f32[8,256]{1,0:T(8,128)S(1)}, f32[8,768,256]{1,2,0:T(8,128)S(1)}) fusion(bf16[512,8,768]{2,1,0:T(8,128)(2,1)} %param.8, bf16[256,512]{1,0:T(8,128)(2,1)S(1)} %copy-done), kind=kOutput, calls=%fused_computation.3 | convolution fusion | flops 1613756416 | bytes 12853248 | tf_op jit(solution)/shard_map/rd,dsv->srv/dot_general | solution.py:80
  14.6 1.9 %pad_add_fusion = s32[8,264,384]{2,1,0:T(8,128)} fusion(s32[8,1,256]{2,1,0:T(1,128)S(1)} %reshape.487, s32[8,256,384]{2,1,0:T(8,128)S(1)} %fusion.3), kind=kLoop, calls=%fused_computation.7 | loop fusion | flops 811008 | bytes 6397952 | tf_op jit(solution)/shard_map/concatenate | solution.py:23
  16.6 4.5 %all-to-all-start = ((s32[8,264,384]{2,1,0:T(8,128)}), s32[8,264,384]{2,1,0:T(8,128)S(1)}, u32[]{:S(2)}, u32[]{:S(2)}) async-start(s32[8,264,384]{2,1,0:T(8,128)} %pad_add_fusion), calls=%async_computation | async-start | bytes 6488064 | tf_op jit(solution)/shard_map/all_to_all | solution.py:81
  22.3 1.3 bitcast_dynamic-update-slice_fusion.9
  23.7 1.3 bitcast_dynamic-update-slice_fusion.8
  25.0 1.3 bitcast_dynamic-update-slice_fusion.7
  26.4 1.5 broadcast_in_dim.98
  27.9 1.5 reshape.479
  30.2 4.0 %collective-permute-start.4 = (bf16[16,2560]{1,0:T(8,128)(2,1)}, bf16[16,2560]{1,0:T(8,128)(2,1)S(1)}, u32[]{:S(2)}, u32[]{:S(2)}) collective-permute-start(bf16[16,2560]{1,0:T(8,128)(2,1)} %reshape.479), channel_id=1, source_target_pairs={{0,16},{8,24},{16,0},{24,8},{1,17},{9,25},{17,1},{25,9},{2,18},{10... | collective-permute-start | bytes 245768 | tf_op jit(solution)/shard_map/ppermute | solution.py:60
  34.2 1.3 collective-permute-start.5
  36.5 24.9 %collective-permute-done.3 = bf16[16,2560]{1,0:T(8,128)(2,1)S(1)} collective-permute-done((bf16[16,2560]{1,0:T(8,128)(2,1)}, bf16[16,2560]{1,0:T(8,128)(2,1)S(1)}, u32[]{:S(2)}, u32[]{:S(2)}) %collective-permute-start.3) | collective-permute-done | bytes 81952 | tf_op jit(solution)/shard_map/ppermute | solution.py:60
  62.4 2.0 %collective-permute-start.6 = (bf16[64,2560]{1,0:T(8,128)(2,1)S(1)}, bf16[64,2560]{1,0:T(8,128)(2,1)S(1)}, u32[]{:S(2)}, u32[]{:S(2)}) collective-permute-start(bf16[64,2560]{1,0:T(8,128)(2,1)S(1)} %bitcast.151), channel_id=1, source_target_pairs={{0,2},{2,4},{4,6},{6,0},{1,3},{3,5},{5,7},{7,1},{8,10},{10,12},{12... | collective-permute-start | bytes 983048 | tf_op jit(solution)/shard_map/ppermute | solution.py:60
  64.4 3.6 %collective-permute-start.7 = (bf16[64,2560]{1,0:T(8,128)(2,1)S(1)}, bf16[64,2560]{1,0:T(8,128)(2,1)S(1)}, u32[]{:S(2)}, u32[]{:S(2)}) collective-permute-start(bf16[64,2560]{1,0:T(8,128)(2,1)S(1)} %bitcast.152), channel_id=1, source_target_pairs={{0,4},{2,6},{4,0},{6,2},{1,5},{3,7},{5,1},{7,3},{8,12},{10,14},{12... | collective-permute-start | bytes 983048 | tf_op jit(solution)/shard_map/ppermute | solution.py:60
  69.0 1.2 broadcast_in_dim.91
  70.9 3.3 %collective-permute-done.6 = bf16[64,2560]{1,0:T(8,128)(2,1)S(1)} collective-permute-done((bf16[64,2560]{1,0:T(8,128)(2,1)S(1)}, bf16[64,2560]{1,0:T(8,128)(2,1)S(1)}, u32[]{:S(2)}, u32[]{:S(2)}) %collective-permute-start.6) | collective-permute-done | bytes 327712 | tf_op jit(solution)/shard_map/ppermute | solution.py:60
  75.1 6.7 %collective-permute-done.7 = bf16[64,2560]{1,0:T(8,128)(2,1)S(1)} collective-permute-done((bf16[64,2560]{1,0:T(8,128)(2,1)S(1)}, bf16[64,2560]{1,0:T(8,128)(2,1)S(1)}, u32[]{:S(2)}, u32[]{:S(2)}) %collective-permute-start.7) | collective-permute-done | bytes 327712 | tf_op jit(solution)/shard_map/ppermute | solution.py:60
  84.1 1.7 %copy.76 = s32[2,4,4,4,2,2]{5,4,3,2,1,0:T(2,128)} copy(s32[2,4,4,4,2,2]{5,0,1,2,3,4:T(2,128)} %bitcast.156) | data formatting | bytes 4096 | tf_op jit(solution)/shard_map/transpose | solution.py:99
  87.1 6.3 %fusion.79 = (f32[512]{0:T(512)S(1)}, f32[512,768]{1,0:T(8,128)}) fusion(bf16[2560,768]{1,0:T(8,128)(2,1)} %param.10, bf16[256,2560]{1,0:T(8,128)(2,1)} %collective-permute-done.9, bf16[256,2560]{1,0:T(8,128)(2,1)} %bitcast.17), kind=kOutput, calls=%fused_computation.172 | convolution fusion | flops 2018901504 | bytes 8128512 | tf_op jit(solution)/shard_map/dot_general | solution.py:88
  95.3 1.5 multiply_reduce_fusion.2
  96.9 12.0 %all_to_all.20 = f32[16,7,512]{2,1,0:T(8,128)S(1)} all-to-all(f32[16,7,512]{2,1,0:T(8,128)S(1)} %broadcast_in_dim.107), channel_id=1, replica_groups=mesh['x'=4,'yh'=2,'yl'=2,'z'=4,'c'=2] {'yl','z','c'}, dimensions={0} | all-to-all | bytes 458752 | tf_op jit(solution)/shard_map/all_to_all | solution.py:67
  109.9 4.8 %all-to-all-start.2 = ((f32[8,7,512]{2,1,0:T(8,128)}), f32[8,7,512]{2,1,0:T(8,128)S(1)}, u32[]{:S(2)}, u32[]{:S(2)}) async-start(f32[8,7,512]{2,1,0:T(8,128)} %broadcast_in_dim.108), calls=%async_computation.2 | async-start | bytes 262144 | tf_op jit(solution)/shard_map/all_to_all | solution.py:67
  114.7 7.9 %all-to-all-done.2 = f32[8,7,512]{2,1,0:T(8,128)S(1)} async-done(((f32[8,7,512]{2,1,0:T(8,128)}), f32[8,7,512]{2,1,0:T(8,128)S(1)}, u32[]{:S(2)}, u32[]{:S(2)}) %all-to-all-start.2) | async-done | bytes 114720 | tf_op jit(solution)/shard_map/all_to_all | solution.py:67
  124.7 1.2 fusion.17
  126.0 4.9 %collective-permute-done.10 = f32[256,2560]{1,0:T(8,128)S(1)} collective-permute-done((f32[256,2560]{1,0:T(8,128)S(1)}, f32[256,2560]{1,0:T(8,128)S(1)}, u32[]{:S(2)}, u32[]{:S(2)}) %collective-permute-start.10) | collective-permute-done | bytes 2621472 | tf_op jit(solution)/shard_map/ppermute | solution.py:147
  130.9 1.2 fusion.2
  132.2 1.2 reshape.485
  133.4 4.9 %all-to-all-start.3 = ((bf16[64,4,2560]{2,1,0:T(4,128)(2,1)}), bf16[64,4,2560]{2,1,0:T(4,128)(2,1)S(1)}, u32[]{:S(2)}, u32[]{:S(2)}) async-start(bf16[64,4,2560]{2,1,0:T(4,128)(2,1)} %reshape.485), calls=%async_computation.3 | async-start | bytes 2621440 | tf_op jit(solution)/shard_map/all_to_all | solution.py:153
  139.5 5.9 %convolution_convert_fusion = bf16[2560,768]{1,0:T(8,128)(2,1)} fusion(bf16[512,768]{1,0:T(8,128)(2,1)S(1)} %copy-done.5, bf16[256,2560]{1,0:T(8,128)(2,1)} %collective-permute-done.9, bf16[256,2560]{1,0:T(8,128)(2,1)} %bitcast.17), kind=kOutput, calls=%fused_computation.4 | convolution fusion | flops 2020474880 | bytes 7340032 | tf_op jit(solution)/shard_map/dot_general | solution.py:149
  145.4 14.9 %all-to-all-done.3 = bf16[64,4,2560]{2,1,0:T(4,128)(2,1)S(1)} async-done(((bf16[64,4,2560]{2,1,0:T(4,128)(2,1)}), bf16[64,4,2560]{2,1,0:T(4,128)(2,1)S(1)}, u32[]{:S(2)}, u32[]{:S(2)}) %all-to-all-start.3) | async-done | bytes 1310752 | tf_op jit(solution)/shard_map/all_to_all | solution.py:153
  (82 shorter events, 20.1 us)
Async XLA Ops:
  0.6 7.2 %copy-start = (bf16[256,512]{1,0:T(8,128)(2,1)S(1)}, bf16[256,512]{1,0:T(8,128)(2,1)}, u32[]{:S(2)}) copy-start(bf16[256,512]{1,0:T(8,128)(2,1)} %param.7) | copy-start | bytes 786436
  2.1 20.3 %collective-permute-start = (bf16[4,2560]{1,0:T(4,128)(2,1)}, bf16[4,2560]{1,0:T(4,128)(2,1)}, u32[]{:S(2)}, u32[]{:S(2)}) collective-permute-start(bf16[4,2560]{1,0:T(4,128)(2,1)} %reshape.478), channel_id=1, source_target_pairs={{0,32},{32,64},{64,96},{96,0},{1,33},{33,65},{65,97},{97,1},{2,34}... | collective-permute-start | bytes 61448 | tf_op jit(solution)/shard_map/ppermute | solution.py:60
  3.6 20.0 %collective-permute-start.1 = (bf16[4,2560]{1,0:T(4,128)(2,1)}, bf16[4,2560]{1,0:T(4,128)(2,1)}, u32[]{:S(2)}, u32[]{:S(2)}) collective-permute-start(bf16[4,2560]{1,0:T(4,128)(2,1)} %reshape.478), channel_id=1, source_target_pairs={{0,64},{32,96},{64,0},{96,32},{1,65},{33,97},{65,1},{97,33},{2,66}... | collective-permute-start | bytes 61448 | tf_op jit(solution)/shard_map/ppermute | solution.py:60
  6.4 18.7 %collective-permute-start.2 = (bf16[4,2560]{1,0:T(4,128)(2,1)}, bf16[4,2560]{1,0:T(4,128)(2,1)}, u32[]{:S(2)}, u32[]{:S(2)}) collective-permute-start(bf16[4,2560]{1,0:T(4,128)(2,1)} %reshape.478), channel_id=1, source_target_pairs={{0,96},{32,0},{64,32},{96,64},{1,97},{33,1},{65,33},{97,65},{2,98}... | collective-permute-start | bytes 61448 | tf_op jit(solution)/shard_map/ppermute | solution.py:60
  16.6 76.8 %all-to-all-start = ((s32[8,264,384]{2,1,0:T(8,128)}), s32[8,264,384]{2,1,0:T(8,128)S(1)}, u32[]{:S(2)}, u32[]{:S(2)}) async-start(s32[8,264,384]{2,1,0:T(8,128)} %pad_add_fusion), calls=%async_computation | async-start | bytes 6488064 | tf_op jit(solution)/shard_map/all_to_all | solution.py:81
  26.4 56.9 %copy-start.6 = (s32[256,2]{0,1:T(2,128)S(1)}, s32[256,2]{0,1:T(2,128)}, u32[]{:S(2)}) copy-start(s32[256,2]{0,1:T(2,128)} %param.11) | copy-start | bytes 6148
  29.4 32.0 %collective-permute-start.3 = (bf16[16,2560]{1,0:T(8,128)(2,1)}, bf16[16,2560]{1,0:T(8,128)(2,1)S(1)}, u32[]{:S(2)}, u32[]{:S(2)}) collective-permute-start(bf16[16,2560]{1,0:T(8,128)(2,1)} %reshape.479), channel_id=1, source_target_pairs={{0,8},{8,16},{16,24},{24,0},{1,9},{9,17},{17,25},{25,1},{2,10},{10... | collective-permute-start | bytes 245768 | tf_op jit(solution)/shard_map/ppermute | solution.py:60
  30.2 32.2 %collective-permute-start.4 = (bf16[16,2560]{1,0:T(8,128)(2,1)}, bf16[16,2560]{1,0:T(8,128)(2,1)S(1)}, u32[]{:S(2)}, u32[]{:S(2)}) collective-permute-start(bf16[16,2560]{1,0:T(8,128)(2,1)} %reshape.479), channel_id=1, source_target_pairs={{0,16},{8,24},{16,0},{24,8},{1,17},{9,25},{17,1},{25,9},{2,18},{10... | collective-permute-start | bytes 245768 | tf_op jit(solution)/shard_map/ppermute | solution.py:60
  34.2 28.2 %collective-permute-start.5 = (bf16[16,2560]{1,0:T(8,128)(2,1)}, bf16[16,2560]{1,0:T(8,128)(2,1)S(1)}, u32[]{:S(2)}, u32[]{:S(2)}) collective-permute-start(bf16[16,2560]{1,0:T(8,128)(2,1)} %reshape.479), channel_id=1, source_target_pairs={{0,24},{8,0},{16,8},{24,16},{1,25},{9,1},{17,9},{25,17},{2,26},{10... | collective-permute-start | bytes 245768 | tf_op jit(solution)/shard_map/ppermute | solution.py:60
  62.4 11.9 %collective-permute-start.6 = (bf16[64,2560]{1,0:T(8,128)(2,1)S(1)}, bf16[64,2560]{1,0:T(8,128)(2,1)S(1)}, u32[]{:S(2)}, u32[]{:S(2)}) collective-permute-start(bf16[64,2560]{1,0:T(8,128)(2,1)S(1)} %bitcast.151), channel_id=1, source_target_pairs={{0,2},{2,4},{4,6},{6,0},{1,3},{3,5},{5,7},{7,1},{8,10},{10,12},{12... | collective-permute-start | bytes 983048 | tf_op jit(solution)/shard_map/ppermute | solution.py:60
  64.4 17.3 %collective-permute-start.7 = (bf16[64,2560]{1,0:T(8,128)(2,1)S(1)}, bf16[64,2560]{1,0:T(8,128)(2,1)S(1)}, u32[]{:S(2)}, u32[]{:S(2)}) collective-permute-start(bf16[64,2560]{1,0:T(8,128)(2,1)S(1)} %bitcast.152), channel_id=1, source_target_pairs={{0,4},{2,6},{4,0},{6,2},{1,5},{3,7},{5,1},{7,3},{8,12},{10,14},{12... | collective-permute-start | bytes 983048 | tf_op jit(solution)/shard_map/ppermute | solution.py:60
  68.0 14.5 %collective-permute-start.8 = (bf16[64,2560]{1,0:T(8,128)(2,1)S(1)}, bf16[64,2560]{1,0:T(8,128)(2,1)S(1)}, u32[]{:S(2)}, u32[]{:S(2)}) collective-permute-start(bf16[64,2560]{1,0:T(8,128)(2,1)S(1)} %bitcast.153), channel_id=1, source_target_pairs={{0,6},{2,0},{4,2},{6,4},{1,7},{3,1},{5,3},{7,5},{8,14},{10,8},{12,... | collective-permute-start | bytes 983048 | tf_op jit(solution)/shard_map/ppermute | solution.py:60
  83.3 3.8 %collective-permute-start.9 = (bf16[256,2560]{1,0:T(8,128)(2,1)}, bf16[256,2560]{1,0:T(8,128)(2,1)}, u32[]{:S(2)}, u32[]{:S(2)}) collective-permute-start(bf16[256,2560]{1,0:T(8,128)(2,1)} %bitcast.17), channel_id=1, source_target_pairs={{0,1},{1,0},{2,3},{3,2},{4,5},{5,4},{6,7},{7,6},{8,9},{9,8},{10,11... | collective-permute-start | bytes 3932168 | tf_op jit(solution)/shard_map/ppermute | solution.py:86
  93.4 1.9 %copy-start.2 = (f32[512,768]{1,0:T(8,128)S(1)}, f32[512,768]{1,0:T(8,128)}, u32[]{:S(2)}) copy-start(f32[512,768]{1,0:T(8,128)} %get-tuple-element.90) | copy-start | bytes 4718596
  95.3 27.6 %copy-start.3 = (f32[512,768]{1,0:T(8,128)S(1)}, f32[512,768]{1,0:T(8,128)}, u32[]{:S(2)}) copy-start(f32[512,768]{1,0:T(8,128)} %get-tuple-element.90) | copy-start | bytes 4718596
  109.9 12.8 %all-to-all-start.2 = ((f32[8,7,512]{2,1,0:T(8,128)}), f32[8,7,512]{2,1,0:T(8,128)S(1)}, u32[]{:S(2)}, u32[]{:S(2)}) async-start(f32[8,7,512]{2,1,0:T(8,128)} %broadcast_in_dim.108), calls=%async_computation.2 | async-start | bytes 262144 | tf_op jit(solution)/shard_map/all_to_all | solution.py:67
  122.6 2.1 %copy-start.1 = (bf16[2560,768]{1,0:T(8,128)(2,1)S(1)}, bf16[2560,768]{1,0:T(8,128)(2,1)}, u32[]{:S(2)}) copy-start(bf16[2560,768]{1,0:T(8,128)(2,1)} %param.10) | copy-start | bytes 11796484
  124.7 6.2 %copy-start.4 = (bf16[512,768]{1,0:T(8,128)(2,1)}, bf16[512,768]{1,0:T(8,128)(2,1)S(1)}, u32[]{:S(2)}) copy-start(bf16[512,768]{1,0:T(8,128)(2,1)S(1)} %fusion.10) | copy-start | bytes 2359300
  126.0 5.0 %collective-permute-start.10 = (f32[256,2560]{1,0:T(8,128)S(1)}, f32[256,2560]{1,0:T(8,128)S(1)}, u32[]{:S(2)}, u32[]{:S(2)}) collective-permute-start(f32[256,2560]{1,0:T(8,128)S(1)} %fusion.17), channel_id=1, source_target_pairs={{0,1},{1,0},{2,3},{3,2},{4,5},{5,4},{6,7},{7,6},{8,9},{9,8},{10,11... | collective-permute-start | bytes 7864328 | tf_op jit(solution)/shard_map/ppermute | solution.py:147
  132.2 7.3 %copy-start.5 = (bf16[512,768]{1,0:T(8,128)(2,1)S(1)}, bf16[512,768]{1,0:T(8,128)(2,1)}, u32[]{:S(2)}) copy-start(bf16[512,768]{1,0:T(8,128)(2,1)} %copy-done.4) | copy-start | bytes 2359300
  133.4 26.9 %all-to-all-start.3 = ((bf16[64,4,2560]{2,1,0:T(4,128)(2,1)}), bf16[64,4,2560]{2,1,0:T(4,128)(2,1)S(1)}, u32[]{:S(2)}, u32[]{:S(2)}) async-start(bf16[64,4,2560]{2,1,0:T(4,128)(2,1)} %reshape.485), calls=%async_computation.3 | async-start | bytes 2621440 | tf_op jit(solution)/shard_map/all_to_all | solution.py:153

commit v3 on v2

--- a/solution.py
+++ b/solution.py
@@ -81,8 +81,8 @@
     words = lax.all_to_all(encode(partial), TOK, 0, 0, tiled=True)
 
     own = jnp.swapaxes(student_hidden, 0, 1).reshape(4, width)
-    for axes in ("x", ("yh", "yl"), "z"):
-        own = ring_gather(own, axes)
+    own = everywhere(own, ("yh", "yl", "x"), 16).reshape(64, width)
+    own = ring_gather(own, "z")
     other = lax.ppermute(own, "c", pair)
     hidden = jnp.concatenate([own, other], axis=0)
     scores = jnp.dot(hidden, student_head, preferred_element_type=jnp.float32)

time: 162 us -> 141 us (0.87)
  waiting for transfers between devices: 63.6 us -> 46.6 us
  starting transfers between devices: 32.8 us -> 28.6 us
  local copies, waits for them, and re-layouts: 22.5 us -> 20.8 us
    ppermute x9 -> x3, waiting for transfers between devices: 35.9 us -> 6.5 us  [ring_gather(): lax.ppermute(block, axes, [(i, (i + step) % size) for i in range(size)])]
    ppermute x9 -> x3, starting transfers between devices: 18.5 us -> 6.51 us  [ring_gather(): lax.ppermute(block, axes, [(i, (i + step) % size) for i in range(size)])]
    all_to_all x1, waiting for transfers between devices: 0.01 us -> 11.5 us  [local(): words = lax.all_to_all(encode(partial), TOK, 0, 0, tiled=True)]
    all_to_all x1 -> x2, starting transfers between devices: 4.85 us -> 10.9 us  [everywhere(): return lax.all_to_all(copies, axes, 0, 0, tiled=True)]
    all_to_all x1, starting transfers between devices: 4.5 us -> 6.47 us  [local(): words = lax.all_to_all(encode(partial), TOK, 0, 0, tiled=True)]
    dynamic_update_slice x9 -> x3, local copies, waits for them, and re-layouts: 6.32 us -> 5.19 us  [ring_gather(): lax.dynamic_update_index_in_dim(whole, taken, (here + size - step) % size...]
    all_to_all x1 -> x2, waiting for transfers between devices: 7.89 us -> 8.48 us  [everywhere(): return lax.all_to_all(copies, axes, 0, 0, tiled=True)]
  transfers between devices with their start and end apart: 14 -> 9, of which waited for: 7 -> 7; matrix products, arithmetic and copies ran while one was open for 24% -> 27% of each run, Pallas kernels for 0% -> 0%
where the time goes in v3:
time: 141 us; the launch traced here: 140 us
  waiting for transfers between devices  46.6 us (33%)
  starting transfers between devices  28.6 us (20%)
  matrix products  21.3 us (15%)
  local copies, waits for them, and re-layouts  20.8 us (15%)
  blocking collectives  13.3 us (9%)
  other arithmetic  8.35 us (6%)
    all_to_all x1, waiting for transfers between devices, local(): share = lax.all_to_all(share, WALK, 0, 0, tiled=True)  15.2 us
    all_to_all x1, blocking collectives, everywhere(): return lax.all_to_all(copies, axes, 0, 0, tiled=True)  13.3 us
    all_to_all x1, waiting for transfers between devices, local(): words = lax.all_to_all(encode(partial), TOK, 0, 0, tiled=True)  11.5 us
    all_to_all x2, starting transfers between devices, everywhere(): return lax.all_to_all(copies, axes, 0, 0, tiled=True)  10.9 us
    all_to_all x2, waiting for transfers between devices, everywhere(): return lax.all_to_all(copies, axes, 0, 0, tiled=True)  8.48 us
    ppermute x3, starting transfers between devices, ring_gather(): lax.ppermute(block, axes, [(i, (i + step) % size) for i in range(size)])  6.51 us
    ppermute x3, waiting for transfers between devices, ring_gather(): lax.ppermute(block, axes, [(i, (i + step) % size) for i in range(size)])  6.5 us
    all_to_all x1, starting transfers between devices, local(): words = lax.all_to_all(encode(partial), TOK, 0, 0, tiled=True)  6.47 us
  transfers between devices with their start and end apart: 9, of which 7 were waited for; matrix products, arithmetic and copies ran while one was open for 27% of the time, Pallas kernels for 0%

profile of v3, /device:TPU:0, one launch (start us, length us, event | category | flops | bytes accessed | tf_op | source)
XLA Modules:
  0.0 139.8 jit_solution(8973274115021441366)
XLA Ops:
  2.3 7.2 %all-to-all-start.1 = ((bf16[16,4,2560]{2,1,0:T(4,128)(2,1)}), bf16[16,4,2560]{2,1,0:T(4,128)(2,1)}, u32[]{:S(2)}, u32[]{:S(2)}) async-start(bf16[16,4,2560]{2,1,0:T(4,128)(2,1)} %broadcast_in_dim.63), calls=%async_computation.1 | async-start | bytes 655360 | tf_op jit(solution)/shard_map/all_to_all | solution.py:67
  9.4 5.7 %abs_reduce_fusion = (f32[8,256]{1,0:T(8,128)S(1)}, f32[8,768,256]{1,2,0:T(8,128)S(1)}) fusion(bf16[512,8,768]{2,1,0:T(8,128)(2,1)} %param.8, bf16[256,512]{1,0:T(8,128)(2,1)S(1)} %copy-done), kind=kOutput, calls=%fused_computation.3 | convolution fusion | flops 1613756416 | bytes 12853248 | tf_op jit(solution)/shard_map/rd,dsv->srv/dot_general | solution.py:80
  16.4 1.9 %pad_add_fusion = s32[8,264,384]{2,1,0:T(8,128)} fusion(s32[8,1,256]{2,1,0:T(1,128)S(1)} %reshape.481, s32[8,256,384]{2,1,0:T(8,128)S(1)} %fusion.3), kind=kLoop, calls=%fused_computation.7 | loop fusion | flops 811008 | bytes 6397952 | tf_op jit(solution)/shard_map/concatenate | solution.py:23
  18.9 6.5 %all-to-all-start = ((s32[8,264,384]{2,1,0:T(8,128)}), s32[8,264,384]{2,1,0:T(8,128)S(1)}, u32[]{:S(2)}, u32[]{:S(2)}) async-start(s32[8,264,384]{2,1,0:T(8,128)} %pad_add_fusion), calls=%async_computation | async-start | bytes 6488064 | tf_op jit(solution)/shard_map/all_to_all | solution.py:81
  25.3 1.8 %reshape.474 = bf16[64,2560]{1,0:T(8,128)(2,1)} reshape(bf16[16,4,2560]{2,1,0:T(4,128)(2,1)} %all-to-all-done.1) | data formatting | bytes 655360 | tf_op jit(solution)/shard_map/reshape | solution.py:84
  27.1 1.9 %collective-permute-start = (bf16[64,2560]{1,0:T(8,128)(2,1)}, bf16[64,2560]{1,0:T(8,128)(2,1)}, u32[]{:S(2)}, u32[]{:S(2)}) collective-permute-start(bf16[64,2560]{1,0:T(8,128)(2,1)} %reshape.474), channel_id=1, source_target_pairs={{0,2},{2,4},{4,6},{6,0},{1,3},{3,5},{5,7},{7,1},{8,10},{10,12},{12... | collective-permute-start | bytes 983048 | tf_op jit(solution)/shard_map/ppermute | solution.py:60
  29.0 3.6 %collective-permute-start.1 = (bf16[64,2560]{1,0:T(8,128)(2,1)}, bf16[64,2560]{1,0:T(8,128)(2,1)}, u32[]{:S(2)}, u32[]{:S(2)}) collective-permute-start(bf16[64,2560]{1,0:T(8,128)(2,1)} %reshape.474), channel_id=1, source_target_pairs={{0,4},{2,6},{4,0},{6,2},{1,5},{3,7},{5,1},{7,3},{8,12},{10,14},{12... | collective-permute-start | bytes 983048 | tf_op jit(solution)/shard_map/ppermute | solution.py:60
  32.6 1.0 collective-permute-start.2
  33.6 1.8 %broadcast_in_dim.64 = bf16[1,64,2560]{2,1,0:T(8,128)(2,1)} reshape(bf16[16,4,2560]{2,1,0:T(4,128)(2,1)} %all-to-all-done.1) | data formatting | bytes 655360 | tf_op jit(solution)/shard_map/jit(dynamic_update_index_in_dim)/broadcast_in_dim | solution.py:58
  35.4 1.2 broadcast_in_dim.62
  36.5 1.7 %constant_dynamic-update-slice_fusion = bf16[4,64,2560]{2,1,0:T(8,128)(2,1)} fusion(bf16[4,64,2560]{2,1,0:T(8,128)(2,1)} %broadcast_in_dim.62, bf16[1,64,2560]{2,1,0:T(8,128)(2,1)} %broadcast_in_dim.64, s32[]{:T(128)S(6)} %select_n.222), kind=kLoop, calls=%fused_computation.148 | loop fusion | bytes 655364 | tf_op jit(solution)/shard_map/jit(dynamic_update_index_in_dim)/dynamic_update_slice | solution.py:58
  39.2 1.7 %bitcast_dynamic-update-slice_fusion.2 = bf16[4,64,2560]{2,1,0:T(8,128)(2,1)} fusion(bf16[4,64,2560]{2,1,0:T(8,128)(2,1)} %constant_dynamic-update-slice_fusion, s32[]{:T(128)S(6)} %select_n.224, bf16[64,2560]{1,0:T(8,128)(2,1)} %collective-permute-done), kind=kLoop, calls=%fused_computation.39 | loop fusion | bytes 655364 | tf_op jit(solution)/shard_map/jit(dynamic_update_index_in_dim)/dynamic_update_slice | solution.py:61
  40.9 5.6 %collective-permute-done.1 = bf16[64,2560]{1,0:T(8,128)(2,1)} collective-permute-done((bf16[64,2560]{1,0:T(8,128)(2,1)}, bf16[64,2560]{1,0:T(8,128)(2,1)}, u32[]{:S(2)}, u32[]{:S(2)}) %collective-permute-start.1) | collective-permute-done | bytes 327712 | tf_op jit(solution)/shard_map/ppermute | solution.py:60
  46.5 1.7 %bitcast_dynamic-update-slice_fusion.1 = bf16[4,64,2560]{2,1,0:T(8,128)(2,1)} fusion(bf16[4,64,2560]{2,1,0:T(8,128)(2,1)} %bitcast_dynamic-update-slice_fusion.2, s32[]{:T(128)S(6)} %select_n.226, bf16[64,2560]{1,0:T(8,128)(2,1)} %collective-permute-done.1), kind=kLoop, calls=%fused_computation.38 | loop fusion | bytes 655364 | tf_op jit(solution)/shard_map/jit(dynamic_update_index_in_dim)/dynamic_update_slice | solution.py:61
  48.3 1.7 %bitcast_dynamic-update-slice_fusion = bf16[4,64,2560]{2,1,0:T(8,128)(2,1)} fusion(bf16[4,64,2560]{2,1,0:T(8,128)(2,1)} %bitcast_dynamic-update-slice_fusion.1, s32[]{:T(128)S(6)} %select_n.228, bf16[64,2560]{1,0:T(8,128)(2,1)} %collective-permute-done.2), kind=kLoop, calls=%fused_computation.37 | loop fusion | bytes 655364 | tf_op jit(solution)/shard_map/jit(dynamic_update_index_in_dim)/dynamic_update_slice | solution.py:61
  50.8 1.7 %copy.71 = s32[2,4,4,4,2,2]{5,4,3,2,1,0:T(2,128)} copy(s32[2,4,4,4,2,2]{5,0,1,2,3,4:T(2,128)} %bitcast.136) | data formatting | bytes 4096 | tf_op jit(solution)/shard_map/transpose | solution.py:99
  52.5 1.1 reshape.477
  53.8 6.3 %fusion.79 = (f32[512]{0:T(512)S(1)}, f32[512,768]{1,0:T(8,128)}) fusion(bf16[2560,768]{1,0:T(8,128)(2,1)} %param.10, bf16[256,2560]{1,0:T(8,128)(2,1)} %collective-permute-done.3, bf16[256,2560]{1,0:T(8,128)(2,1)} %bitcast.9), kind=kOutput, calls=%fused_computation.164 | convolution fusion | flops 2018901504 | bytes 8128512 | tf_op jit(solution)/shard_map/dot_general | solution.py:88
  60.0 11.5 %all-to-all-done = s32[8,264,384]{2,1,0:T(8,128)S(1)} async-done(((s32[8,264,384]{2,1,0:T(8,128)}), s32[8,264,384]{2,1,0:T(8,128)S(1)}, u32[]{:S(2)}, u32[]{:S(2)}) %all-to-all-start) | async-done | bytes 3244064 | tf_op jit(solution)/shard_map/all_to_all | solution.py:81
  72.5 1.0 fusion.78
  73.5 1.5 %multiply_reduce_fusion.2 = (f32[512]{0:T(512)S(1)}, f32[512]{0:T(512)S(1)}, f32[512]{0:T(512)S(1)}, f32[512]{0:T(512)S(1)}, f32[512]{0:T(512)S(1)}) fusion(f32[512,768]{1,0:T(8,128)S(1)} %get-tuple-element.88, f32[512,768]{1,0:T(8,128)S(1)} %copy-done.2, f32[512]{0:T(512)S(1)} %get-tuple-element.87, s32[512]{0:T(512)S(1)} %bitcast.139, ...), kind=kLoop, calls=%fused_computation.23 | loop fusion | flops 5502464 | bytes 3165184 | tf_op jit(solution)/shard_map/reduce_sum | solution.py:117
  75.1 13.3 %all_to_all.25 = f32[16,7,512]{2,1,0:T(8,128)S(1)} all-to-all(f32[16,7,512]{2,1,0:T(8,128)S(1)} %broadcast_in_dim.69), channel_id=1, replica_groups=mesh['x'=4,'yh'=2,'yl'=2,'z'=4,'c'=2] {'yl','z','c'}, dimensions={0} | all-to-all | bytes 458752 | tf_op jit(solution)/shard_map/all_to_all | solution.py:67
  89.3 3.7 %all-to-all-start.3 = ((f32[8,7,512]{2,1,0:T(8,128)}), f32[8,7,512]{2,1,0:T(8,128)S(1)}, u32[]{:S(2)}, u32[]{:S(2)}) async-start(f32[8,7,512]{2,1,0:T(8,128)} %broadcast_in_dim.70), calls=%async_computation.3 | async-start | bytes 262144 | tf_op jit(solution)/shard_map/all_to_all | solution.py:67
  93.1 7.9 %all-to-all-done.3 = f32[8,7,512]{2,1,0:T(8,128)S(1)} async-done(((f32[8,7,512]{2,1,0:T(8,128)}), f32[8,7,512]{2,1,0:T(8,128)S(1)}, u32[]{:S(2)}, u32[]{:S(2)}) %all-to-all-start.3) | async-done | bytes 114720 | tf_op jit(solution)/shard_map/all_to_all | solution.py:67
  101.2 1.1 fusion.10
  103.1 1.2 fusion.17
  104.4 4.9 %collective-permute-done.4 = f32[256,2560]{1,0:T(8,128)S(1)} collective-permute-done((f32[256,2560]{1,0:T(8,128)S(1)}, f32[256,2560]{1,0:T(8,128)S(1)}, u32[]{:S(2)}, u32[]{:S(2)}) %collective-permute-start.4) | collective-permute-done | bytes 2621472 | tf_op jit(solution)/shard_map/ppermute | solution.py:147
  109.3 1.2 fusion.2
  110.5 1.2 reshape.479
  111.7 4.7 %all-to-all-start.4 = ((bf16[64,4,2560]{2,1,0:T(4,128)(2,1)}), bf16[64,4,2560]{2,1,0:T(4,128)(2,1)S(1)}, u32[]{:S(2)}, u32[]{:S(2)}) async-start(bf16[64,4,2560]{2,1,0:T(4,128)(2,1)} %reshape.479), calls=%async_computation.4 | async-start | bytes 2621440 | tf_op jit(solution)/shard_map/all_to_all | solution.py:153
  117.6 5.9 %convolution_convert_fusion = bf16[2560,768]{1,0:T(8,128)(2,1)} fusion(bf16[512,768]{1,0:T(8,128)(2,1)S(1)} %copy-done.5, bf16[256,2560]{1,0:T(8,128)(2,1)} %collective-permute-done.3, bf16[256,2560]{1,0:T(8,128)(2,1)} %bitcast.9), kind=kOutput, calls=%fused_computation.4 | convolution fusion | flops 2020474880 | bytes 7340032 | tf_op jit(solution)/shard_map/dot_general | solution.py:149
  123.5 15.2 %all-to-all-done.4 = bf16[64,4,2560]{2,1,0:T(4,128)(2,1)S(1)} async-done(((bf16[64,4,2560]{2,1,0:T(4,128)(2,1)}), bf16[64,4,2560]{2,1,0:T(4,128)(2,1)S(1)}, u32[]{:S(2)}, u32[]{:S(2)}) %all-to-all-start.4) | async-done | bytes 1310752 | tf_op jit(solution)/shard_map/all_to_all | solution.py:153
  (62 shorter events, 10.6 us)
Async XLA Ops:
  0.6 8.8 %copy-start = (bf16[256,512]{1,0:T(8,128)(2,1)S(1)}, bf16[256,512]{1,0:T(8,128)(2,1)}, u32[]{:S(2)}) copy-start(bf16[256,512]{1,0:T(8,128)(2,1)} %param.7) | copy-start | bytes 786436
  2.3 16.6 %all-to-all-start.1 = ((bf16[16,4,2560]{2,1,0:T(4,128)(2,1)}), bf16[16,4,2560]{2,1,0:T(4,128)(2,1)}, u32[]{:S(2)}, u32[]{:S(2)}) async-start(bf16[16,4,2560]{2,1,0:T(4,128)(2,1)} %broadcast_in_dim.63), calls=%async_computation.1 | async-start | bytes 655360 | tf_op jit(solution)/shard_map/all_to_all | solution.py:67
  18.9 52.7 %all-to-all-start = ((s32[8,264,384]{2,1,0:T(8,128)}), s32[8,264,384]{2,1,0:T(8,128)S(1)}, u32[]{:S(2)}, u32[]{:S(2)}) async-start(s32[8,264,384]{2,1,0:T(8,128)} %pad_add_fusion), calls=%async_computation | async-start | bytes 6488064 | tf_op jit(solution)/shard_map/all_to_all | solution.py:81
  25.3 24.6 %copy-start.6 = (s32[256,2]{0,1:T(2,128)S(1)}, s32[256,2]{0,1:T(2,128)}, u32[]{:S(2)}) copy-start(s32[256,2]{0,1:T(2,128)} %param.11) | copy-start | bytes 6148
  27.1 12.1 %collective-permute-start = (bf16[64,2560]{1,0:T(8,128)(2,1)}, bf16[64,2560]{1,0:T(8,128)(2,1)}, u32[]{:S(2)}, u32[]{:S(2)}) collective-permute-start(bf16[64,2560]{1,0:T(8,128)(2,1)} %reshape.474), channel_id=1, source_target_pairs={{0,2},{2,4},{4,6},{6,0},{1,3},{3,5},{5,7},{7,1},{8,10},{10,12},{12... | collective-permute-start | bytes 983048 | tf_op jit(solution)/shard_map/ppermute | solution.py:60
  29.0 17.5 %collective-permute-start.1 = (bf16[64,2560]{1,0:T(8,128)(2,1)}, bf16[64,2560]{1,0:T(8,128)(2,1)}, u32[]{:S(2)}, u32[]{:S(2)}) collective-permute-start(bf16[64,2560]{1,0:T(8,128)(2,1)} %reshape.474), channel_id=1, source_target_pairs={{0,4},{2,6},{4,0},{6,2},{1,5},{3,7},{5,1},{7,3},{8,12},{10,14},{12... | collective-permute-start | bytes 983048 | tf_op jit(solution)/shard_map/ppermute | solution.py:60
  32.6 15.6 %collective-permute-start.2 = (bf16[64,2560]{1,0:T(8,128)(2,1)}, bf16[64,2560]{1,0:T(8,128)(2,1)}, u32[]{:S(2)}, u32[]{:S(2)}) collective-permute-start(bf16[64,2560]{1,0:T(8,128)(2,1)} %reshape.474), channel_id=1, source_target_pairs={{0,6},{2,0},{4,2},{6,4},{1,7},{3,1},{5,3},{7,5},{8,14},{10,8},{12,... | collective-permute-start | bytes 983048 | tf_op jit(solution)/shard_map/ppermute | solution.py:60
  50.0 3.8 %collective-permute-start.3 = (bf16[256,2560]{1,0:T(8,128)(2,1)}, bf16[256,2560]{1,0:T(8,128)(2,1)}, u32[]{:S(2)}, u32[]{:S(2)}) collective-permute-start(bf16[256,2560]{1,0:T(8,128)(2,1)} %bitcast.9), channel_id=1, source_target_pairs={{0,1},{1,0},{2,3},{3,2},{4,5},{5,4},{6,7},{7,6},{8,9},{9,8},{10,11... | collective-permute-start | bytes 3932168 | tf_op jit(solution)/shard_map/ppermute | solution.py:86
  71.6 1.9 %copy-start.2 = (f32[512,768]{1,0:T(8,128)S(1)}, f32[512,768]{1,0:T(8,128)}, u32[]{:S(2)}) copy-start(f32[512,768]{1,0:T(8,128)} %get-tuple-element.90) | copy-start | bytes 4718596
  73.5 27.7 %copy-start.3 = (f32[512,768]{1,0:T(8,128)S(1)}, f32[512,768]{1,0:T(8,128)}, u32[]{:S(2)}) copy-start(f32[512,768]{1,0:T(8,128)} %get-tuple-element.90) | copy-start | bytes 4718596
  89.3 11.6 %all-to-all-start.3 = ((f32[8,7,512]{2,1,0:T(8,128)}), f32[8,7,512]{2,1,0:T(8,128)S(1)}, u32[]{:S(2)}, u32[]{:S(2)}) async-start(f32[8,7,512]{2,1,0:T(8,128)} %broadcast_in_dim.70), calls=%async_computation.3 | async-start | bytes 262144 | tf_op jit(solution)/shard_map/all_to_all | solution.py:67
  100.9 2.1 %copy-start.1 = (bf16[2560,768]{1,0:T(8,128)(2,1)S(1)}, bf16[2560,768]{1,0:T(8,128)(2,1)}, u32[]{:S(2)}) copy-start(bf16[2560,768]{1,0:T(8,128)(2,1)} %param.10) | copy-start | bytes 11796484
  103.1 6.2 %copy-start.4 = (bf16[512,768]{1,0:T(8,128)(2,1)}, bf16[512,768]{1,0:T(8,128)(2,1)S(1)}, u32[]{:S(2)}) copy-start(bf16[512,768]{1,0:T(8,128)(2,1)S(1)} %fusion.10) | copy-start | bytes 2359300
  104.3 5.0 %collective-permute-start.4 = (f32[256,2560]{1,0:T(8,128)S(1)}, f32[256,2560]{1,0:T(8,128)S(1)}, u32[]{:S(2)}, u32[]{:S(2)}) collective-permute-start(f32[256,2560]{1,0:T(8,128)S(1)} %fusion.17), channel_id=1, source_target_pairs={{0,1},{1,0},{2,3},{3,2},{4,5},{5,4},{6,7},{7,6},{8,9},{9,8},{10,11... | collective-permute-start | bytes 7864328 | tf_op jit(solution)/shard_map/ppermute | solution.py:147
  110.5 7.1 %copy-start.5 = (bf16[512,768]{1,0:T(8,128)(2,1)S(1)}, bf16[512,768]{1,0:T(8,128)(2,1)}, u32[]{:S(2)}) copy-start(bf16[512,768]{1,0:T(8,128)(2,1)} %copy-done.4) | copy-start | bytes 2359300
  111.7 26.9 %all-to-all-start.4 = ((bf16[64,4,2560]{2,1,0:T(4,128)(2,1)}), bf16[64,4,2560]{2,1,0:T(4,128)(2,1)S(1)}, u32[]{:S(2)}, u32[]{:S(2)}) async-start(bf16[64,4,2560]{2,1,0:T(4,128)(2,1)} %reshape.479), calls=%async_computation.4 | async-start | bytes 2621440 | tf_op jit(solution)/shard_map/all_to_all | solution.py:153

commit v4 on v3

--- a/solution.py
+++ b/solution.py
@@ -4,11 +4,11 @@
 from jax.sharding import Mesh
 from jax.sharding import PartitionSpec as P
 
-TOK = ("x", "yh")
+TOK = ("xh", "xl", "yh")
 VOC = ("yl", "z", "c")
-CHIPS = ("x", "yh", "yl", "z")
-SIZES = (4, 2, 2, 4, 2)
-WALK = ("z", "yh", "yl", "x")
+SIZES = (2, 2, 2, 2, 4, 2)
+STRIPES = ("yh", "xl", "xh")
+WALK = ("z", "yh", "yl", "xh", "xl")
 
 
 def encode(partial):
@@ -69,7 +69,7 @@
 
 def local(teacher_hidden, teacher_head, student_hidden, student_head, target_ids):
     core = lax.axis_index("c")
-    chips = lax.axis_size(CHIPS)
+    chips = lax.axis_size(WALK)
     stripes = teacher_head.shape[1]
     voc = teacher_head.shape[2]
     rows = teacher_hidden.shape[0]
@@ -78,10 +78,12 @@
     pair = [(0, 1), (1, 0)]
 
     partial = jnp.einsum("rd,dsv->srv", teacher_hidden, teacher_head, preferred_element_type=jnp.float32)
-    words = lax.all_to_all(encode(partial), TOK, 0, 0, tiled=True)
+    words = encode(partial)
+    words = words.reshape((2, 2, 2) + words.shape[1:]).transpose(2, 1, 0, 3, 4).reshape(words.shape)
+    words = lax.all_to_all(words, STRIPES, 0, 0, tiled=True)
 
     own = jnp.swapaxes(student_hidden, 0, 1).reshape(4, width)
-    own = everywhere(own, ("yh", "yl", "x"), 16).reshape(64, width)
+    own = everywhere(own, ("yh", "yl", "xh", "xl"), 16).reshape(64, width)
     own = ring_gather(own, "z")
     other = lax.ppermute(own, "c", pair)
     hidden = jnp.concatenate([own, other], axis=0)
@@ -150,6 +152,7 @@
         hidden, grad, (((0,), (0,)), ((), ())), preferred_element_type=jnp.float32
     ).astype(jnp.bfloat16)
     share = (keep + taken).astype(jnp.bfloat16).reshape(chips, 4, width)
+    share, grad_head = lax.optimization_barrier((share, grad_head))
     share = lax.all_to_all(share, WALK, 0, 0, tiled=True)
     grad_hidden = jnp.sum(share.astype(jnp.float32), axis=0).astype(jnp.bfloat16)
     grad_hidden = jnp.swapaxes(grad_hidden.reshape(2, 2, width), 0, 1)
@@ -157,7 +160,7 @@
 
 
 def solution(mesh):
-    fine = Mesh(mesh.devices.reshape(SIZES), CHIPS + ("c",))
+    fine = Mesh(mesh.devices.reshape(SIZES), TOK + VOC)
     return jax.shard_map(
         local,
         mesh=fine,

time: 141 us -> 144 us (1.021)
  starting transfers between devices: 28.6 us -> 36.2 us
  waiting for transfers between devices: 46.6 us -> 41.6 us
  local copies, waits for them, and re-layouts: 20.8 us -> 22.7 us
  other arithmetic: 8.35 us -> 6.66 us
    all_to_all x2, starting transfers between devices: 10.9 us -> 18.2 us  [everywhere(): return lax.all_to_all(copies, axes, 0, 0, tiled=True)]
    all_to_all x1, waiting for transfers between devices: 15.2 us -> 21.4 us  [local(): share = lax.all_to_all(share, WALK, 0, 0, tiled=True)]
    all_to_all x1, waiting for transfers between devices: 11.5 us -> 5.47 us  [local(): words = lax.all_to_all(words, STRIPES, 0, 0, tiled=True)]
    ppermute x1, waiting for transfers between devices: 4.9 us -> 0.01 us  [local(): taken = lax.ppermute(give, 'c', pair)]
    transpose x0 -> x1, local copies, waits for them, and re-layouts: none -> 1.91 us  [local(): words.reshape((2, 2, 2) + words.shape[1:]).transpose(2, 1, 0, 3, 4)]
    concatenate x1, other arithmetic: 1.91 us -> 0.21 us  [encode(): return jnp.concatenate([words, tail], axis=1)]
  transfers between devices with their start and end apart: 9 -> 9, of which waited for: 7 -> 6; matrix products, arithmetic and copies ran while one was open for 27% -> 26% of each run, Pallas kernels for 0% -> 0%
where the time goes in v4:
time: 144 us; the launch traced here: 143 us
  waiting for transfers between devices  41.6 us (29%)
  starting transfers between devices  36.2 us (25%)
  local copies, waits for them, and re-layouts  22.7 us (16%)
  matrix products  21.3 us (15%)
  blocking collectives  13.3 us (9%)
  other arithmetic  6.66 us (5%)
    all_to_all x1, waiting for transfers between devices, local(): share = lax.all_to_all(share, WALK, 0, 0, tiled=True)  21.4 us
    all_to_all x2, starting transfers between devices, everywhere(): return lax.all_to_all(copies, axes, 0, 0, tiled=True)  18.2 us
    all_to_all x1, blocking collectives, everywhere(): return lax.all_to_all(copies, axes, 0, 0, tiled=True)  13.3 us
    all_to_all x2, waiting for transfers between devices, everywhere(): return lax.all_to_all(copies, axes, 0, 0, tiled=True)  8.28 us
    all_to_all x1, starting transfers between devices, local(): words = lax.all_to_all(words, STRIPES, 0, 0, tiled=True)  6.67 us
    ppermute x3, starting transfers between devices, ring_gather(): lax.ppermute(block, axes, [(i, (i + step) % size) for i in range(size)])  6.51 us
    ppermute x3, waiting for transfers between devices, ring_gather(): lax.ppermute(block, axes, [(i, (i + step) % size) for i in range(size)])  6.5 us
    dot_general x1, matrix products, local(): scores = jnp.dot(hidden, student_head, preferred_element_type=jnp.float32)  6.27 us
  transfers between devices with their start and end apart: 9, of which 6 were waited for; matrix products, arithmetic and copies ran while one was open for 26% of the time, Pallas kernels for 0%

profile of v4, /device:TPU:0, one launch (start us, length us, event | category | flops | bytes accessed | tf_op | source)
XLA Modules:
  0.0 142.7 jit_solution(17960148382978392361)
XLA Ops:
  2.3 7.2 %all-to-all-start.1 = ((bf16[16,4,2560]{2,1,0:T(4,128)(2,1)}), bf16[16,4,2560]{2,1,0:T(4,128)(2,1)}, u32[]{:S(2)}, u32[]{:S(2)}) async-start(bf16[16,4,2560]{2,1,0:T(4,128)(2,1)} %broadcast_in_dim.63), calls=%async_computation.1 | async-start | bytes 655360 | tf_op jit(solution)/shard_map/all_to_all | solution.py:67
  9.4 5.7 %abs_reduce_fusion = (f32[8,256]{1,0:T(8,128)S(1)}, f32[8,768,256]{1,2,0:T(8,128)S(1)}) fusion(bf16[512,8,768]{2,1,0:T(8,128)(2,1)} %param.8, bf16[256,512]{1,0:T(8,128)(2,1)S(1)} %copy-done), kind=kOutput, calls=%fused_computation.3 | convolution fusion | flops 1613756416 | bytes 12853248 | tf_op jit(solution)/shard_map/rd,dsv->srv/dot_general | solution.py:80
  16.6 1.9 %copy.74 = s32[2,2,2,264,384]{4,3,2,1,0:T(8,128)} copy(s32[2,2,2,264,384]{4,3,0,1,2:T(8,128)S(1)} %bitcast.139) | data formatting | bytes 6488064 | tf_op jit(solution)/shard_map/transpose | solution.py:82
  18.9 6.7 %all-to-all-start = ((s32[8,264,384]{2,1,0:T(8,128)}), s32[8,264,384]{2,1,0:T(8,128)S(1)}, u32[]{:S(2)}, u32[]{:S(2)}) async-start(s32[8,264,384]{2,1,0:T(8,128)} %bitcast.4), calls=%async_computation | async-start | bytes 6488064 | tf_op jit(solution)/shard_map/all_to_all | solution.py:83
  25.5 1.8 %reshape.482 = bf16[64,2560]{1,0:T(8,128)(2,1)} reshape(bf16[16,4,2560]{2,1,0:T(4,128)(2,1)} %all-to-all-done.1) | data formatting | bytes 655360 | tf_op jit(solution)/shard_map/reshape | solution.py:86
  27.3 1.9 %collective-permute-start = (bf16[64,2560]{1,0:T(8,128)(2,1)}, bf16[64,2560]{1,0:T(8,128)(2,1)}, u32[]{:S(2)}, u32[]{:S(2)}) collective-permute-start(bf16[64,2560]{1,0:T(8,128)(2,1)} %reshape.482), channel_id=1, source_target_pairs={{0,2},{2,4},{4,6},{6,0},{1,3},{3,5},{5,7},{7,1},{8,10},{10,12},{12... | collective-permute-start | bytes 983048 | tf_op jit(solution)/shard_map/ppermute | solution.py:60
  29.2 3.6 %collective-permute-start.1 = (bf16[64,2560]{1,0:T(8,128)(2,1)}, bf16[64,2560]{1,0:T(8,128)(2,1)}, u32[]{:S(2)}, u32[]{:S(2)}) collective-permute-start(bf16[64,2560]{1,0:T(8,128)(2,1)} %reshape.482), channel_id=1, source_target_pairs={{0,4},{2,6},{4,0},{6,2},{1,5},{3,7},{5,1},{7,3},{8,12},{10,14},{12... | collective-permute-start | bytes 983048 | tf_op jit(solution)/shard_map/ppermute | solution.py:60
  32.8 1.0 collective-permute-start.2
  33.8 1.8 %broadcast_in_dim.64 = bf16[1,64,2560]{2,1,0:T(8,128)(2,1)} reshape(bf16[16,4,2560]{2,1,0:T(4,128)(2,1)} %all-to-all-done.1) | data formatting | bytes 655360 | tf_op jit(solution)/shard_map/jit(dynamic_update_index_in_dim)/broadcast_in_dim | solution.py:58
  35.6 1.2 broadcast_in_dim.62
  36.7 1.7 %constant_dynamic-update-slice_fusion = bf16[4,64,2560]{2,1,0:T(8,128)(2,1)} fusion(bf16[4,64,2560]{2,1,0:T(8,128)(2,1)} %broadcast_in_dim.62, bf16[1,64,2560]{2,1,0:T(8,128)(2,1)} %broadcast_in_dim.64, s32[]{:T(128)S(6)} %select_n.222), kind=kLoop, calls=%fused_computation.148 | loop fusion | bytes 655364 | tf_op jit(solution)/shard_map/jit(dynamic_update_index_in_dim)/dynamic_update_slice | solution.py:58
  39.4 1.7 %bitcast_dynamic-update-slice_fusion.2 = bf16[4,64,2560]{2,1,0:T(8,128)(2,1)} fusion(bf16[4,64,2560]{2,1,0:T(8,128)(2,1)} %constant_dynamic-update-slice_fusion, s32[]{:T(128)S(6)} %select_n.224, bf16[64,2560]{1,0:T(8,128)(2,1)} %collective-permute-done), kind=kLoop, calls=%fused_computation.39 | loop fusion | bytes 655364 | tf_op jit(solution)/shard_map/jit(dynamic_update_index_in_dim)/dynamic_update_slice | solution.py:61
  41.1 5.6 %collective-permute-done.1 = bf16[64,2560]{1,0:T(8,128)(2,1)} collective-permute-done((bf16[64,2560]{1,0:T(8,128)(2,1)}, bf16[64,2560]{1,0:T(8,128)(2,1)}, u32[]{:S(2)}, u32[]{:S(2)}) %collective-permute-start.1) | collective-permute-done | bytes 327712 | tf_op jit(solution)/shard_map/ppermute | solution.py:60
  46.7 1.7 %bitcast_dynamic-update-slice_fusion.1 = bf16[4,64,2560]{2,1,0:T(8,128)(2,1)} fusion(bf16[4,64,2560]{2,1,0:T(8,128)(2,1)} %bitcast_dynamic-update-slice_fusion.2, s32[]{:T(128)S(6)} %select_n.226, bf16[64,2560]{1,0:T(8,128)(2,1)} %collective-permute-done.1), kind=kLoop, calls=%fused_computation.38 | loop fusion | bytes 655364 | tf_op jit(solution)/shard_map/jit(dynamic_update_index_in_dim)/dynamic_update_slice | solution.py:61
  48.5 1.7 %bitcast_dynamic-update-slice_fusion = bf16[4,64,2560]{2,1,0:T(8,128)(2,1)} fusion(bf16[4,64,2560]{2,1,0:T(8,128)(2,1)} %bitcast_dynamic-update-slice_fusion.1, s32[]{:T(128)S(6)} %select_n.228, bf16[64,2560]{1,0:T(8,128)(2,1)} %collective-permute-done.2), kind=kLoop, calls=%fused_computation.37 | loop fusion | bytes 655364 | tf_op jit(solution)/shard_map/jit(dynamic_update_index_in_dim)/dynamic_update_slice | solution.py:61
  51.0 1.7 %copy.77 = s32[2,4,4,4,2,2]{5,4,3,2,1,0:T(2,128)} copy(s32[2,4,4,4,2,2]{5,0,1,2,3,4:T(2,128)} %bitcast.141) | data formatting | bytes 4096 | tf_op jit(solution)/shard_map/transpose | solution.py:101
  52.7 1.1 reshape.485
  54.0 6.3 %fusion.79 = (f32[512]{0:T(512)S(1)}, f32[512,768]{1,0:T(8,128)}) fusion(bf16[2560,768]{1,0:T(8,128)(2,1)} %param.10, bf16[256,2560]{1,0:T(8,128)(2,1)} %collective-permute-done.3, bf16[256,2560]{1,0:T(8,128)(2,1)} %bitcast.12), kind=kOutput, calls=%fused_computation.164 | convolution fusion | flops 2018901504 | bytes 8128512 | tf_op jit(solution)/shard_map/dot_general | solution.py:90
  60.2 5.5 %all-to-all-done = s32[8,264,384]{2,1,0:T(8,128)S(1)} async-done(((s32[8,264,384]{2,1,0:T(8,128)}), s32[8,264,384]{2,1,0:T(8,128)S(1)}, u32[]{:S(2)}, u32[]{:S(2)}) %all-to-all-start) | async-done | bytes 3244064 | tf_op jit(solution)/shard_map/all_to_all | solution.py:83
  65.7 0.9 multiply_reduce_fusion.1
  66.7 1.0 fusion.78
  67.7 1.5 %multiply_reduce_fusion.2 = (f32[512]{0:T(512)S(1)}, f32[512]{0:T(512)S(1)}, f32[512]{0:T(512)S(1)}, f32[512]{0:T(512)S(1)}, f32[512]{0:T(512)S(1)}) fusion(f32[512,768]{1,0:T(8,128)S(1)} %get-tuple-element.92, f32[512,768]{1,0:T(8,128)S(1)} %copy-done.2, f32[512]{0:T(512)S(1)} %get-tuple-element.91, s32[512]{0:T(512)S(1)} %bitcast.144, ...), kind=kLoop, calls=%fused_computation.23 | loop fusion | flops 5502464 | bytes 3165184 | tf_op jit(solution)/shard_map/reduce_sum | solution.py:119
  69.3 13.3 %all_to_all.25 = f32[16,7,512]{2,1,0:T(8,128)S(1)} all-to-all(f32[16,7,512]{2,1,0:T(8,128)S(1)} %broadcast_in_dim.69), channel_id=1, replica_groups=mesh['xh'=2,'xl'=2,'yh'=2,'yl'=2,'z'=4,'c'=2] {'yl','z','c'}, dimensions={0} | all-to-all | bytes 458752 | tf_op jit(solution)/shard_map/all_to_all | solution.py:67
  83.5 11.1 %all-to-all-start.3 = ((f32[8,7,512]{2,1,0:T(8,128)}), f32[8,7,512]{2,1,0:T(8,128)S(1)}, u32[]{:S(2)}, u32[]{:S(2)}) async-start(f32[8,7,512]{2,1,0:T(8,128)} %broadcast_in_dim.70), calls=%async_computation.3 | async-start | bytes 262144 | tf_op jit(solution)/shard_map/all_to_all | solution.py:67
  94.6 7.9 %all-to-all-done.3 = f32[8,7,512]{2,1,0:T(8,128)S(1)} async-done(((f32[8,7,512]{2,1,0:T(8,128)}), f32[8,7,512]{2,1,0:T(8,128)S(1)}, u32[]{:S(2)}, u32[]{:S(2)}) %all-to-all-start.3) | async-done | bytes 114720 | tf_op jit(solution)/shard_map/all_to_all | solution.py:67
  102.8 1.1 fusion.10
  104.6 1.2 fusion.17
  105.9 5.9 %convolution_convert_fusion = bf16[2560,768]{1,0:T(8,128)(2,1)} fusion(bf16[512,768]{1,0:T(8,128)(2,1)S(1)} %fusion.10, bf16[256,2560]{1,0:T(8,128)(2,1)} %collective-permute-done.3, bf16[256,2560]{1,0:T(8,128)(2,1)} %bitcast.12), kind=kOutput, calls=%fused_computation.4 | convolution fusion | flops 2020474880 | bytes 7340032 | tf_op jit(solution)/shard_map/dot_general | solution.py:151
  111.8 1.2 fusion.2
  113.0 1.2 reshape.487
  114.3 4.7 %all-to-all-start.4 = ((bf16[64,4,2560]{2,1,0:T(4,128)(2,1)}), bf16[64,4,2560]{2,1,0:T(4,128)(2,1)S(1)}, u32[]{:S(2)}, u32[]{:S(2)}) async-start(bf16[64,4,2560]{2,1,0:T(4,128)(2,1)} %reshape.487), calls=%async_computation.4 | async-start | bytes 2621440 | tf_op jit(solution)/shard_map/all_to_all | solution.py:156
  120.1 21.4 %all-to-all-done.4 = bf16[64,4,2560]{2,1,0:T(4,128)(2,1)S(1)} async-done(((bf16[64,4,2560]{2,1,0:T(4,128)(2,1)}), bf16[64,4,2560]{2,1,0:T(4,128)(2,1)S(1)}, u32[]{:S(2)}, u32[]{:S(2)}) %all-to-all-start.4) | async-done | bytes 1310752 | tf_op jit(solution)/shard_map/all_to_all | solution.py:156
  (59 shorter events, 9.7 us)
Async XLA Ops:
  0.6 8.8 %copy-start = (bf16[256,512]{1,0:T(8,128)(2,1)S(1)}, bf16[256,512]{1,0:T(8,128)(2,1)}, u32[]{:S(2)}) copy-start(bf16[256,512]{1,0:T(8,128)(2,1)} %param.7) | copy-start | bytes 786436
  2.3 16.6 %all-to-all-start.1 = ((bf16[16,4,2560]{2,1,0:T(4,128)(2,1)}), bf16[16,4,2560]{2,1,0:T(4,128)(2,1)}, u32[]{:S(2)}, u32[]{:S(2)}) async-start(bf16[16,4,2560]{2,1,0:T(4,128)(2,1)} %broadcast_in_dim.63), calls=%async_computation.1 | async-start | bytes 655360 | tf_op jit(solution)/shard_map/all_to_all | solution.py:67
  18.9 46.8 %all-to-all-start = ((s32[8,264,384]{2,1,0:T(8,128)}), s32[8,264,384]{2,1,0:T(8,128)S(1)}, u32[]{:S(2)}, u32[]{:S(2)}) async-start(s32[8,264,384]{2,1,0:T(8,128)} %bitcast.4), calls=%async_computation | async-start | bytes 6488064 | tf_op jit(solution)/shard_map/all_to_all | solution.py:83
  25.5 24.6 %copy-start.4 = (s32[256,2]{0,1:T(2,128)S(1)}, s32[256,2]{0,1:T(2,128)}, u32[]{:S(2)}) copy-start(s32[256,2]{0,1:T(2,128)} %param.11) | copy-start | bytes 6148
  27.3 12.1 %collective-permute-start = (bf16[64,2560]{1,0:T(8,128)(2,1)}, bf16[64,2560]{1,0:T(8,128)(2,1)}, u32[]{:S(2)}, u32[]{:S(2)}) collective-permute-start(bf16[64,2560]{1,0:T(8,128)(2,1)} %reshape.482), channel_id=1, source_target_pairs={{0,2},{2,4},{4,6},{6,0},{1,3},{3,5},{5,7},{7,1},{8,10},{10,12},{12... | collective-permute-start | bytes 983048 | tf_op jit(solution)/shard_map/ppermute | solution.py:60
  29.2 17.5 %collective-permute-start.1 = (bf16[64,2560]{1,0:T(8,128)(2,1)}, bf16[64,2560]{1,0:T(8,128)(2,1)}, u32[]{:S(2)}, u32[]{:S(2)}) collective-permute-start(bf16[64,2560]{1,0:T(8,128)(2,1)} %reshape.482), channel_id=1, source_target_pairs={{0,4},{2,6},{4,0},{6,2},{1,5},{3,7},{5,1},{7,3},{8,12},{10,14},{12... | collective-permute-start | bytes 983048 | tf_op jit(solution)/shard_map/ppermute | solution.py:60
  32.8 15.6 %collective-permute-start.2 = (bf16[64,2560]{1,0:T(8,128)(2,1)}, bf16[64,2560]{1,0:T(8,128)(2,1)}, u32[]{:S(2)}, u32[]{:S(2)}) collective-permute-start(bf16[64,2560]{1,0:T(8,128)(2,1)} %reshape.482), channel_id=1, source_target_pairs={{0,6},{2,0},{4,2},{6,4},{1,7},{3,1},{5,3},{7,5},{8,14},{10,8},{12,... | collective-permute-start | bytes 983048 | tf_op jit(solution)/shard_map/ppermute | solution.py:60
  50.2 3.8 %collective-permute-start.3 = (bf16[256,2560]{1,0:T(8,128)(2,1)}, bf16[256,2560]{1,0:T(8,128)(2,1)}, u32[]{:S(2)}, u32[]{:S(2)}) collective-permute-start(bf16[256,2560]{1,0:T(8,128)(2,1)} %bitcast.12), channel_id=1, source_target_pairs={{0,1},{1,0},{2,3},{3,2},{4,5},{5,4},{6,7},{7,6},{8,9},{9,8},{10,11... | collective-permute-start | bytes 3932168 | tf_op jit(solution)/shard_map/ppermute | solution.py:88
  65.7 1.9 %copy-start.2 = (f32[512,768]{1,0:T(8,128)S(1)}, f32[512,768]{1,0:T(8,128)}, u32[]{:S(2)}) copy-start(f32[512,768]{1,0:T(8,128)} %get-tuple-element.94) | copy-start | bytes 4718596
  67.7 35.1 %copy-start.3 = (f32[512,768]{1,0:T(8,128)S(1)}, f32[512,768]{1,0:T(8,128)}, u32[]{:S(2)}) copy-start(f32[512,768]{1,0:T(8,128)} %get-tuple-element.94) | copy-start | bytes 4718596
  83.5 19.0 %all-to-all-start.3 = ((f32[8,7,512]{2,1,0:T(8,128)}), f32[8,7,512]{2,1,0:T(8,128)S(1)}, u32[]{:S(2)}, u32[]{:S(2)}) async-start(f32[8,7,512]{2,1,0:T(8,128)} %broadcast_in_dim.70), calls=%async_computation.3 | async-start | bytes 262144 | tf_op jit(solution)/shard_map/all_to_all | solution.py:67
  102.5 2.1 %copy-start.1 = (bf16[2560,768]{1,0:T(8,128)(2,1)S(1)}, bf16[2560,768]{1,0:T(8,128)(2,1)}, u32[]{:S(2)}) copy-start(bf16[2560,768]{1,0:T(8,128)(2,1)} %param.10) | copy-start | bytes 11796484
  105.8 6.0 %collective-permute-start.4 = (f32[256,2560]{1,0:T(8,128)S(1)}, f32[256,2560]{1,0:T(8,128)S(1)}, u32[]{:S(2)}, u32[]{:S(2)}) collective-permute-start(f32[256,2560]{1,0:T(8,128)S(1)} %fusion.17), channel_id=1, source_target_pairs={{0,1},{1,0},{2,3},{3,2},{4,5},{5,4},{6,7},{7,6},{8,9},{9,8},{10,11... | collective-permute-start | bytes 7864328 | tf_op jit(solution)/shard_map/ppermute | solution.py:149
  114.3 27.3 %all-to-all-start.4 = ((bf16[64,4,2560]{2,1,0:T(4,128)(2,1)}), bf16[64,4,2560]{2,1,0:T(4,128)(2,1)S(1)}, u32[]{:S(2)}, u32[]{:S(2)}) async-start(bf16[64,4,2560]{2,1,0:T(4,128)(2,1)} %reshape.487), calls=%async_computation.4 | async-start | bytes 2621440 | tf_op jit(solution)/shard_map/all_to_all | solution.py:156

commit v5 on v4

--- a/solution.py
+++ b/solution.py
@@ -7,29 +7,27 @@
 TOK = ("xh", "xl", "yh")
 VOC = ("yl", "z", "c")
 SIZES = (2, 2, 2, 2, 4, 2)
-STRIPES = ("yh", "xl", "xh")
+STEPS = ((2, 1), (1, 1), (3, 1), (2, 0), (0, 1), (1, 0), (3, 0))
 WALK = ("z", "yh", "yl", "xh", "xl")
 
 
-def encode(partial):
-    stripes, rows, width = partial.shape
+def encode(partial, level):
+    rows, width = partial.shape
     half = width // 2
-    peak = jnp.maximum(jnp.max(jnp.abs(partial), axis=2), 1e-30)
-    level = jnp.ceil(jnp.log2(peak) * 256.0)
-    scale = jnp.exp2(-level / 256.0) * 32766.0
-    code = jnp.clip(jnp.round(partial * scale[:, :, None]), -32767.0, 32767.0).astype(jnp.int32)
-    words = (code[:, :, :half] << 16) | (code[:, :, half:] & 0xFFFF)
-    tail = jnp.zeros((stripes, 8, half), jnp.int32).at[:, 0, :rows].set(level.astype(jnp.int32))
-    return jnp.concatenate([words, tail], axis=1)
+    scale = jnp.exp2(level * (-1.0 / 256.0)) * 32766.0
+    code = jnp.clip(jnp.round(partial * scale[:, None]), -32767.0, 32767.0).astype(jnp.int32)
+    words = (code[:, :half] << 16) | (code[:, half:] & 0xFFFF)
+    tail = jnp.pad(level.astype(jnp.int32)[None], ((0, 7), (0, half - rows)))
+    return jnp.concatenate([words, tail], axis=0)
 
 
 def decode(words, rows):
-    level = words[:, rows, :rows].astype(jnp.float32)
-    scale = (jnp.exp2(level / 256.0) * (0.5 / 32766.0))[:, :, None]
-    body = words[:, :rows]
+    level = words[rows, :rows].astype(jnp.float32)
+    scale = (jnp.exp2(level * (1.0 / 256.0)) * (0.5 / 32766.0))[:, None]
+    body = words[:rows]
     high = (body >> 16).astype(jnp.float32)
     low = ((body << 16) >> 16).astype(jnp.float32)
-    return jnp.concatenate([jnp.sum(high * scale, axis=0), jnp.sum(low * scale, axis=0)], axis=1)
+    return high * scale, low * scale
 
 
 def merge(parts):
@@ -78,9 +76,20 @@
     pair = [(0, 1), (1, 0)]
 
     partial = jnp.einsum("rd,dsv->srv", teacher_hidden, teacher_head, preferred_element_type=jnp.float32)
-    words = encode(partial)
-    words = words.reshape((2, 2, 2) + words.shape[1:]).transpose(2, 1, 0, 3, 4).reshape(words.shape)
-    words = lax.all_to_all(words, STRIPES, 0, 0, tiled=True)
+    peak = jnp.maximum(jnp.max(jnp.abs(partial), axis=2), 1e-30)
+    level = jnp.ceil(jnp.log2(peak) * 256.0)
+    tok = lax.axis_index(TOK)
+
+    def move(index, step):
+        return (index // 2 + step[0]) % 4 * 2 + (index % 2 + step[1]) % 2
+
+    arrived = []
+    for step in STEPS:
+        to = move(tok, step)
+        words = encode(
+            lax.dynamic_index_in_dim(partial, to, 0, False), lax.dynamic_index_in_dim(level, to, 0, False)
+        )
+        arrived.append(lax.ppermute(words, TOK, [(i, move(i, step)) for i in range(stripes)]))
 
     own = jnp.swapaxes(student_hidden, 0, 1).reshape(4, width)
     own = everywhere(own, ("yh", "yl", "xh", "xl"), 16).reshape(64, width)
@@ -103,7 +112,10 @@
     match = lax.broadcasted_iota(jnp.int32, (1, voc), 1) + base == ids
 
     pick = (lax.broadcasted_iota(jnp.int32, (1, rows), 1) == teacher_row).astype(jnp.float32)
-    teacher = jnp.dot(pick, decode(words, rows), precision=lax.Precision.HIGHEST)
+    parts = [decode(words, rows) for words in arrived]
+    whole = jnp.concatenate([sum(p[0] for p in parts), sum(p[1] for p in parts)], axis=1)
+    whole = whole + 0.5 * lax.dynamic_index_in_dim(partial, tok, 0, False)
+    teacher = jnp.dot(pick, whole, precision=lax.Precision.HIGHEST)
 
     t_peak = jnp.max(teacher, axis=1, keepdims=True)
     t_exp = jnp.exp(teacher - t_peak)
@@ -152,7 +164,7 @@
         hidden, grad, (((0,), (0,)), ((), ())), preferred_element_type=jnp.float32
     ).astype(jnp.bfloat16)
     share = (keep + taken).astype(jnp.bfloat16).reshape(chips, 4, width)
-    share, grad_head = lax.optimization_barrier((share, grad_head))
+    share, grad_head, objective = lax.optimization_barrier((share, grad_head, objective))
     share = lax.all_to_all(share, WALK, 0, 0, tiled=True)
     grad_hidden = jnp.sum(share.astype(jnp.float32), axis=0).astype(jnp.bfloat16)
     grad_hidden = jnp.swapaxes(grad_hidden.reshape(2, 2, width), 0, 1)

time: 144 us -> 163 us (1.13)
  blocking collectives: 13.3 us -> 39.2 us
  local copies, waits for them, and re-layouts: 22.7 us -> 5.88 us
  other arithmetic: 6.66 us -> 17.6 us
  matrix products: 21.3 us -> 23.2 us
    all_to_all x2 -> x0, waiting for transfers between devices: 26.9 us -> none  [the longest x1 21.4 us: local(): share = lax.all_to_all(share, WALK, 0, 0, tiled=True)]
    all_to_all x0 -> x1, blocking collectives: none -> 26.4 us  [local(): share = lax.all_to_all(share, WALK, 0, 0, tiled=True)]
    all_to_all x2, waiting for transfers between devices: 8.28 us -> 30.3 us  [everywhere(): return lax.all_to_all(copies, axes, 0, 0, tiled=True)]
    ppermute x0 -> x7, starting transfers between devices: none -> 15.1 us  [local(): lax.ppermute(words, TOK, [(i, move(i, step)) for i in range(stripes)])]
    all_to_all x2 -> x0, starting transfers between devices: 11.3 us -> none  [the longest x1 6.67 us: local(): words = lax.all_to_all(words, STRIPES, 0, 0, tiled=True)]
    all_to_all x2, starting transfers between devices: 18.2 us -> 12.7 us  [everywhere(): return lax.all_to_all(copies, axes, 0, 0, tiled=True)]
    dynamic_update_slice x3, local copies, waits for them, and re-layouts: 5.19 us -> 0.08 us  [ring_gather(): lax.dynamic_update_index_in_dim(whole, taken, (here + size - step) % size...]
    dot_general x1, matrix products: 6.27 us -> 2.27 us  [local(): scores = jnp.dot(hidden, student_head, preferred_element_type=jnp.float32)]
  transfers between devices with their start and end apart: 9 -> 14, of which waited for: 6 -> 5; matrix products, arithmetic and copies ran while one was open for 26% -> 13% of each run, Pallas kernels for 0% -> 0%
where the time goes in v5:
time: 163 us; the launch traced here: 162 us
  waiting for transfers between devices  40 us (25%)
  blocking collectives  39.2 us (24%)
  starting transfers between devices  34.8 us (21%)
  matrix products  23.2 us (14%)
  other arithmetic  17.6 us (11%)
  local copies, waits for them, and re-layouts  5.88 us (4%)
    all_to_all x2, waiting for transfers between devices, everywhere(): return lax.all_to_all(copies, axes, 0, 0, tiled=True)  30.3 us
    all_to_all x1, blocking collectives, local(): share = lax.all_to_all(share, WALK, 0, 0, tiled=True)  26.4 us
    ppermute x7, starting transfers between devices, local(): lax.ppermute(words, TOK, [(i, move(i, step)) for i in range(stripes)])  15.1 us
    all_to_all x1, blocking collectives, everywhere(): return lax.all_to_all(copies, axes, 0, 0, tiled=True)  12.7 us
    all_to_all x2, starting transfers between devices, everywhere(): return lax.all_to_all(copies, axes, 0, 0, tiled=True)  12.7 us
    ppermute x3, waiting for transfers between devices, ring_gather(): lax.ppermute(block, axes, [(i, (i + step) % size) for i in range(size)])  9.68 us
    dot_general x1, matrix products, local(): jnp.einsum('rd,dsv->srv', teacher_hidden, teacher_head, preferred_element...  8.28 us
    ppermute x3, starting transfers between devices, ring_gather(): lax.ppermute(block, axes, [(i, (i + step) % size) for i in range(size)])  6.65 us
  transfers between devices with their start and end apart: 14, of which 5 were waited for; matrix products, arithmetic and copies ran while one was open for 13% of the time, Pallas kernels for 0%

profile of v5, /device:TPU:0, one launch (start us, length us, event | category | flops | bytes accessed | tf_op | source)
XLA Modules:
  0.0 162.0 jit_solution(3387208079947725361)
XLA Ops:
  0.8 0.8 copy-done
  1.6 8.3 %abs_reduce_fusion = (f32[8,256]{1,0:T(8,128)S(1)}, f32[8,768,256]{1,2,0:T(8,128)}) fusion(bf16[512,8,768]{2,1,0:T(8,128)(2,1)} %param.6, bf16[256,512]{1,0:T(8,128)(2,1)S(1)} %copy-done), kind=kOutput, calls=%fused_computation.2 | convolution fusion | flops 1613756416 | bytes 12853248 | tf_op jit(solution)/shard_map/rd,dsv->srv/dot_general | solution.py:78
  10.0 3.2 %fusion.36 = (s32[256,768]{1,0:T(8,128)S(1)}, s32[256,768]{1,0:T(8,128)S(1)}, s32[256,768]{1,0:T(8,128)S(1)}, s32[256,768]{1,0:T(8,128)S(1)}, s32[256,768]{1,0:T...) fusion(f32[8,768,256]{1,2,0:T(8,128)} %get-tuple-element.91, s32[]{:T(128)S(6)} %select_n.334, ...), kind=kLoop, calls=%fused_computation.54 | loop fusion | flops 5505024 | bytes 11017244 | tf_op jit(solution)/shard_map/convert_element_type | solution.py:18
  13.2 0.8 pad_add_fusion.6
  14.0 5.7 %collective-permute-start.4 = (s32[264,384]{1,0:T(8,128)}, s32[264,384]{1,0:T(8,128)S(1)}, u32[]{:S(2)}, u32[]{:S(2)}) collective-permute-start(s32[264,384]{1,0:T(8,128)} %pad_add_fusion.6), channel_id=1, source_target_pairs={{0,80},{16,64},{32,112},{48,96},{64,16},{80,0},{96,48},{112,32},{1... | collective-permute-start | bytes 1216520 | tf_op jit(solution)/shard_map/ppermute | solution.py:92
  19.8 0.8 pad_add_fusion.5
  21.8 5.3 %collective-permute-start.6 = (s32[264,384]{1,0:T(8,128)}, s32[264,384]{1,0:T(8,128)}, u32[]{:S(2)}, u32[]{:S(2)}) collective-permute-start(s32[264,384]{1,0:T(8,128)} %pad_add_fusion.4), channel_id=1, source_target_pairs={{0,112},{16,96},{32,16},{48,0},{64,48},{80,32},{96,80},{112,64},{1... | collective-permute-start | bytes 1216520 | tf_op jit(solution)/shard_map/ppermute | solution.py:92
  27.1 0.8 pad_add_fusion.3
  28.0 0.8 pad_add_fusion.2
  29.1 0.8 broadcast_in_dim.82
  30.0 7.7 %all-to-all-start = ((bf16[16,4,2560]{2,1,0:T(4,128)(2,1)}), bf16[16,4,2560]{2,1,0:T(4,128)(2,1)S(1)}, u32[]{:S(2)}, u32[]{:S(2)}) async-start(bf16[16,4,2560]{2,1,0:T(4,128)(2,1)} %broadcast_in_dim.82), calls=%async_computation | async-start | bytes 655360 | tf_op jit(solution)/shard_map/all_to_all | solution.py:65
  38.6 22.4 %all-to-all-done = bf16[16,4,2560]{2,1,0:T(4,128)(2,1)S(1)} async-done(((bf16[16,4,2560]{2,1,0:T(4,128)(2,1)}), bf16[16,4,2560]{2,1,0:T(4,128)(2,1)S(1)}, u32[]{:S(2)}, u32[]{:S(2)}) %all-to-all-start) | async-done | bytes 327712 | tf_op jit(solution)/shard_map/all_to_all | solution.py:65
  61.4 3.3 %collective-permute-start.10 = (s32[264,384]{1,0:T(8,128)S(1)}, s32[264,384]{1,0:T(8,128)S(1)}, u32[]{:S(2)}, u32[]{:S(2)}) collective-permute-start(s32[264,384]{1,0:T(8,128)S(1)} %pad_add_fusion), channel_id=1, source_target_pairs={{0,96},{16,112},{32,0},{48,16},{64,32},{80,48},{96,64},{112,80},{1... | collective-permute-start | bytes 1216520 | tf_op jit(solution)/shard_map/ppermute | solution.py:92
  64.7 1.9 %collective-permute-start = (bf16[64,2560]{1,0:T(8,128)(2,1)S(1)}, bf16[64,2560]{1,0:T(8,128)(2,1)S(1)}, u32[]{:S(2)}, u32[]{:S(2)}) collective-permute-start(bf16[64,2560]{1,0:T(8,128)(2,1)S(1)} %reshape.579), channel_id=1, source_target_pairs={{0,2},{2,4},{4,6},{6,0},{1,3},{3,5},{5,7},{7,1},{8,10},{10,12},{12... | collective-permute-start | bytes 983048 | tf_op jit(solution)/shard_map/ppermute | solution.py:58
  67.3 3.7 %collective-permute-start.1 = (bf16[64,2560]{1,0:T(8,128)(2,1)S(1)}, bf16[64,2560]{1,0:T(8,128)(2,1)S(1)}, u32[]{:S(2)}, u32[]{:S(2)}) collective-permute-start(bf16[64,2560]{1,0:T(8,128)(2,1)S(1)} %reshape.579), channel_id=1, source_target_pairs={{0,4},{2,6},{4,0},{6,2},{1,5},{3,7},{5,1},{7,3},{8,12},{10,14},{12... | collective-permute-start | bytes 983048 | tf_op jit(solution)/shard_map/ppermute | solution.py:58
  71.7 1.1 collective-permute-start.2
  73.5 3.0 %collective-permute-done = bf16[64,2560]{1,0:T(8,128)(2,1)S(1)} collective-permute-done((bf16[64,2560]{1,0:T(8,128)(2,1)S(1)}, bf16[64,2560]{1,0:T(8,128)(2,1)S(1)}, u32[]{:S(2)}, u32[]{:S(2)}) %collective-permute-start) | collective-permute-done | bytes 327712 | tf_op jit(solution)/shard_map/ppermute | solution.py:58
  76.5 6.5 %collective-permute-done.1 = bf16[64,2560]{1,0:T(8,128)(2,1)S(1)} collective-permute-done((bf16[64,2560]{1,0:T(8,128)(2,1)S(1)}, bf16[64,2560]{1,0:T(8,128)(2,1)S(1)}, u32[]{:S(2)}, u32[]{:S(2)}) %collective-permute-start.1) | collective-permute-done | bytes 327712 | tf_op jit(solution)/shard_map/ppermute | solution.py:58
  83.6 1.8 %multiply_add_fusion.1 = f32[256,384]{1,0:T(8,128)S(1)} fusion(s32[264,384]{1,0:T(8,128)S(1)} %collective-permute-done.10, s32[264,384]{1,0:T(8,128)S(1)} %collective-permute-done.9, s32[264,384]{1,0:T(8,128)} %collective-permute-done.8, s32[264,384]{1,0:T(8,128)} %collective-permute-done.7, s32[264,384]{1,0:T(8,128)} %collective-permute-done.6, ...), kind=kLoop, calls=%fused_computation.91 | loop fusion | flops 2654208 | bytes 3152896 | tf_op jit(solution)/shard_map/add | solution.py:116
  85.4 1.9 %multiply_add_fusion = f32[256,384]{1,0:T(8,128)S(1)} fusion(s32[264,384]{1,0:T(8,128)S(1)} %collective-permute-done.10, s32[264,384]{1,0:T(8,128)S(1)} %collective-permute-done.9, s32[264,384]{1,0:T(8,128)} %collective-permute-done.8, s32[264,384]{1,0:T(8,128)} %collective-permute-done.7, s32[264,384]{1,0:T(8,128)} %collective-permute-done.6, ...), kind=kLoop, calls=%fused_computation.90 | loop fusion | flops 3342336 | bytes 3152896 | tf_op jit(solution)/shard_map/add | solution.py:116
  87.2 2.2 %fusion.133 = (f32[512]{0:T(512)S(1)}, f32[512,768]{1,0:T(8,128)S(1)}) fusion(f32[256,384]{1,0:T(8,128)S(1)} %multiply_add_fusion, f32[256,384]{1,0:T(8,128)S(1)} %multiply_add_fusion.1, f32[8,768,256]{1,2,0:T(8,128)} %get-tuple-element.91, s32[]{:T(128)S(6)} %select_n.345, s32[512]{0:T(512)S(1)} %add_minimum_fusion), kind=kOutput, calls=%fused_computation.262 | convolution fusion | flops 1209073152 | bytes 3149828 | tf_op jit(solution)/shard_map/dot_general | solution.py:118
  89.5 2.3 %fusion.134 = (f32[512]{0:T(512)S(1)}, f32[512,768]{1,0:T(8,128)S(1)}) fusion(bf16[2560,768]{1,0:T(8,128)(2,1)S(1)} %copy-done.1, bf16[256,2560]{1,0:T(8,128)(2,1)S(1)} %collective-permute-done.3, bf16[256,2560]{1,0:T(8,128)(2,1)S(1)} %bitcast.225), kind=kOutput, calls=%fused_computation.263 | convolution fusion | flops 2018901504 | bytes 8128512 | tf_op jit(solution)/shard_map/dot_general | solution.py:99
  91.7 1.4 multiply_reduce_fusion
  93.3 12.7 %all_to_all.20 = f32[16,7,512]{2,1,0:T(8,128)S(1)} all-to-all(f32[16,7,512]{2,1,0:T(8,128)S(1)} %broadcast_in_dim.88), channel_id=1, replica_groups=mesh['xh'=2,'xl'=2,'yh'=2,'yl'=2,'z'=4,'c'=2] {'yl','z','c'}, dimensions={0} | all-to-all | bytes 458752 | tf_op jit(solution)/shard_map/all_to_all | solution.py:65
  106.9 5.0 %all-to-all-start.2 = ((f32[8,7,512]{2,1,0:T(8,128)}), f32[8,7,512]{2,1,0:T(8,128)S(1)}, u32[]{:S(2)}, u32[]{:S(2)}) async-start(f32[8,7,512]{2,1,0:T(8,128)} %broadcast_in_dim.89), calls=%async_computation.2 | async-start | bytes 262144 | tf_op jit(solution)/shard_map/all_to_all | solution.py:65
  112.0 7.9 %all-to-all-done.2 = f32[8,7,512]{2,1,0:T(8,128)S(1)} async-done(((f32[8,7,512]{2,1,0:T(8,128)}), f32[8,7,512]{2,1,0:T(8,128)S(1)}, u32[]{:S(2)}, u32[]{:S(2)}) %all-to-all-start.2) | async-done | bytes 114720 | tf_op jit(solution)/shard_map/all_to_all | solution.py:65
  120.2 1.1 fusion.9
  121.3 1.0 copy-done.2
  122.3 1.2 fusion.39
  124.8 6.2 %convolution_convert_fusion = bf16[2560,768]{1,0:T(8,128)(2,1)} fusion(bf16[512,768]{1,0:T(8,128)(2,1)} %copy-done.4, bf16[256,2560]{1,0:T(8,128)(2,1)} %copy-done.9, bf16[256,2560]{1,0:T(8,128)(2,1)} %bitcast.226), kind=kOutput, calls=%fused_computation.3 | convolution fusion | flops 2020474880 | bytes 7340032 | tf_op jit(solution)/shard_map/dot_general | solution.py:163
  131.0 3.0 %fusion.2 = bf16[256,2560]{1,0:T(8,128)(2,1)S(1)} fusion(f32[256,2560]{1,0:T(8,128)} %collective-permute-done.11, bf16[2560,768]{1,0:T(8,128)(2,1)S(1)} %copy-done.3, bf16[512,768]{1,0:T(8,128)(2,1)S(1)} %copy-done.5), kind=kOutput, calls=%fused_computation.5 | convolution fusion | flops 1007943680 | bytes 8257536 | tf_op jit(solution)/shard_map/dot_general | solution.py:162
  134.4 26.4 %all_to_all.21 = bf16[64,4,2560]{2,1,0:T(4,128)(2,1)S(1)} all-to-all(bf16[64,4,2560]{2,1,0:T(4,128)(2,1)S(1)} %reshape.583), channel_id=1, replica_groups=mesh['xh'=2,'xl'=2,'yh'=2,'yl'=2,'z'=4,'c'=2] {'z','yh','yl','xh','xl'}, dimensions={0} | all-to-all | bytes 2621440 | tf_op jit(solution)/shard_map/all_to_all | solution.py:168
  (97 shorter events, 9.7 us)
Async XLA Ops:
  0.6 1.0 copy-start
  14.0 47.3 %collective-permute-start.4 = (s32[264,384]{1,0:T(8,128)}, s32[264,384]{1,0:T(8,128)S(1)}, u32[]{:S(2)}, u32[]{:S(2)}) collective-permute-start(s32[264,384]{1,0:T(8,128)} %pad_add_fusion.6), channel_id=1, source_target_pairs={{0,80},{16,64},{32,112},{48,96},{64,16},{80,0},{96,48},{112,32},{1... | collective-permute-start | bytes 1216520 | tf_op jit(solution)/shard_map/ppermute | solution.py:92
  20.6 40.8 %collective-permute-start.5 = (s32[264,384]{1,0:T(8,128)}, s32[264,384]{1,0:T(8,128)S(1)}, u32[]{:S(2)}, u32[]{:S(2)}) collective-permute-start(s32[264,384]{1,0:T(8,128)} %pad_add_fusion.5), channel_id=1, source_target_pairs={{0,48},{16,32},{32,80},{48,64},{64,112},{80,96},{96,16},{112,0},{1... | collective-permute-start | bytes 1216520 | tf_op jit(solution)/shard_map/ppermute | solution.py:92
  21.8 42.9 %collective-permute-start.6 = (s32[264,384]{1,0:T(8,128)}, s32[264,384]{1,0:T(8,128)}, u32[]{:S(2)}, u32[]{:S(2)}) collective-permute-start(s32[264,384]{1,0:T(8,128)} %pad_add_fusion.4), channel_id=1, source_target_pairs={{0,112},{16,96},{32,16},{48,0},{64,48},{80,32},{96,80},{112,64},{1... | collective-permute-start | bytes 1216520 | tf_op jit(solution)/shard_map/ppermute | solution.py:92
  27.1 2.0 %copy-start.7 = (bf16[2,2,2560]{2,1,0:T(2,128)(2,1)S(1)}, bf16[2,2,2560]{2,1,0:T(2,128)(2,1)}, u32[]{:S(2)}) copy-start(bf16[2,2,2560]{2,1,0:T(2,128)(2,1)} %param.7) | copy-start | bytes 61444
  27.9 39.4 %collective-permute-start.7 = (s32[264,384]{1,0:T(8,128)}, s32[264,384]{1,0:T(8,128)}, u32[]{:S(2)}, u32[]{:S(2)}) collective-permute-start(s32[264,384]{1,0:T(8,128)} %pad_add_fusion.3), channel_id=1, source_target_pairs={{0,64},{16,80},{32,96},{48,112},{64,0},{80,16},{96,32},{112,48},{1... | collective-permute-start | bytes 1216520 | tf_op jit(solution)/shard_map/ppermute | solution.py:92
  28.7 43.0 %collective-permute-start.8 = (s32[264,384]{1,0:T(8,128)}, s32[264,384]{1,0:T(8,128)}, u32[]{:S(2)}, u32[]{:S(2)}) collective-permute-start(s32[264,384]{1,0:T(8,128)} %pad_add_fusion.2), channel_id=1, source_target_pairs={{0,16},{16,0},{32,48},{48,32},{64,80},{80,64},{96,112},{112,96},{1... | collective-permute-start | bytes 1216520 | tf_op jit(solution)/shard_map/ppermute | solution.py:92
  30.0 7.8 %copy-start.8 = (s32[256,2]{0,1:T(2,128)S(1)}, s32[256,2]{0,1:T(2,128)}, u32[]{:S(2)}) copy-start(s32[256,2]{0,1:T(2,128)} %param.9) | copy-start | bytes 6148
  30.0 31.0 %all-to-all-start = ((bf16[16,4,2560]{2,1,0:T(4,128)(2,1)}), bf16[16,4,2560]{2,1,0:T(4,128)(2,1)S(1)}, u32[]{:S(2)}, u32[]{:S(2)}) async-start(bf16[16,4,2560]{2,1,0:T(4,128)(2,1)} %broadcast_in_dim.82), calls=%async_computation | async-start | bytes 655360 | tf_op jit(solution)/shard_map/all_to_all | solution.py:65
  61.3 22.2 %collective-permute-start.9 = (s32[264,384]{1,0:T(8,128)S(1)}, s32[264,384]{1,0:T(8,128)S(1)}, u32[]{:S(2)}, u32[]{:S(2)}) collective-permute-start(s32[264,384]{1,0:T(8,128)S(1)} %pad_add_fusion.1), channel_id=1, source_target_pairs={{0,32},{16,48},{32,64},{48,80},{64,96},{80,112},{96,0},{112,16},{1... | collective-permute-start | bytes 1216520 | tf_op jit(solution)/shard_map/ppermute | solution.py:92
  61.4 22.2 %collective-permute-start.10 = (s32[264,384]{1,0:T(8,128)S(1)}, s32[264,384]{1,0:T(8,128)S(1)}, u32[]{:S(2)}, u32[]{:S(2)}) collective-permute-start(s32[264,384]{1,0:T(8,128)S(1)} %pad_add_fusion), channel_id=1, source_target_pairs={{0,96},{16,112},{32,0},{48,16},{64,32},{80,48},{96,64},{112,80},{1... | collective-permute-start | bytes 1216520 | tf_op jit(solution)/shard_map/ppermute | solution.py:92
  64.7 11.8 %collective-permute-start = (bf16[64,2560]{1,0:T(8,128)(2,1)S(1)}, bf16[64,2560]{1,0:T(8,128)(2,1)S(1)}, u32[]{:S(2)}, u32[]{:S(2)}) collective-permute-start(bf16[64,2560]{1,0:T(8,128)(2,1)S(1)} %reshape.579), channel_id=1, source_target_pairs={{0,2},{2,4},{4,6},{6,0},{1,3},{3,5},{5,7},{7,1},{8,10},{10,12},{12... | collective-permute-start | bytes 983048 | tf_op jit(solution)/shard_map/ppermute | solution.py:58
  67.3 15.7 %collective-permute-start.1 = (bf16[64,2560]{1,0:T(8,128)(2,1)S(1)}, bf16[64,2560]{1,0:T(8,128)(2,1)S(1)}, u32[]{:S(2)}, u32[]{:S(2)}) collective-permute-start(bf16[64,2560]{1,0:T(8,128)(2,1)S(1)} %reshape.579), channel_id=1, source_target_pairs={{0,4},{2,6},{4,0},{6,2},{1,5},{3,7},{5,1},{7,3},{8,12},{10,14},{12... | collective-permute-start | bytes 983048 | tf_op jit(solution)/shard_map/ppermute | solution.py:58
  71.7 11.5 %collective-permute-start.2 = (bf16[64,2560]{1,0:T(8,128)(2,1)S(1)}, bf16[64,2560]{1,0:T(8,128)(2,1)S(1)}, u32[]{:S(2)}, u32[]{:S(2)}) collective-permute-start(bf16[64,2560]{1,0:T(8,128)(2,1)S(1)} %reshape.579), channel_id=1, source_target_pairs={{0,6},{2,0},{4,2},{6,4},{1,7},{3,1},{5,3},{7,5},{8,14},{10,8},{12,... | collective-permute-start | bytes 983048 | tf_op jit(solution)/shard_map/ppermute | solution.py:58
  83.2 6.2 %copy-start.6 = (bf16[4,64,2560]{2,1,0:T(8,128)(2,1)}, bf16[4,64,2560]{2,1,0:T(8,128)(2,1)S(1)}, u32[]{:S(2)}) copy-start(bf16[4,64,2560]{2,1,0:T(8,128)(2,1)S(1)} %bitcast_dynamic-update-slice_fusion) | copy-start | bytes 3932164
  83.3 6.2 %collective-permute-start.3 = (bf16[256,2560]{1,0:T(8,128)(2,1)S(1)}, bf16[256,2560]{1,0:T(8,128)(2,1)S(1)}, u32[]{:S(2)}, u32[]{:S(2)}) collective-permute-start(bf16[256,2560]{1,0:T(8,128)(2,1)S(1)} %bitcast.224), channel_id=1, source_target_pairs={{0,1},{1,0},{2,3},{3,2},{4,5},{5,4},{6,7},{7,6},{8,9},{9,8},{10,11... | collective-permute-start | bytes 3932168 | tf_op jit(solution)/shard_map/ppermute | solution.py:97
  85.3 4.1 %copy-start.1 = (bf16[2560,768]{1,0:T(8,128)(2,1)S(1)}, bf16[2560,768]{1,0:T(8,128)(2,1)}, u32[]{:S(2)}) copy-start(bf16[2560,768]{1,0:T(8,128)(2,1)} %param.8) | copy-start | bytes 11796484
  89.5 2.3 %copy-start.9 = (bf16[256,2560]{1,0:T(8,128)(2,1)}, bf16[256,2560]{1,0:T(8,128)(2,1)S(1)}, u32[]{:S(2)}) copy-start(bf16[256,2560]{1,0:T(8,128)(2,1)S(1)} %collective-permute-done.3) | copy-start | bytes 3932164
  106.9 12.9 %all-to-all-start.2 = ((f32[8,7,512]{2,1,0:T(8,128)}), f32[8,7,512]{2,1,0:T(8,128)S(1)}, u32[]{:S(2)}, u32[]{:S(2)}) async-start(f32[8,7,512]{2,1,0:T(8,128)} %broadcast_in_dim.89), calls=%async_computation.2 | async-start | bytes 262144 | tf_op jit(solution)/shard_map/all_to_all | solution.py:65
  120.1 2.1 %copy-start.2 = (bf16[2560,768]{1,0:T(8,128)(2,1)S(1)}, bf16[2560,768]{1,0:T(8,128)(2,1)}, u32[]{:S(2)}) copy-start(bf16[2560,768]{1,0:T(8,128)(2,1)} %param.8) | copy-start | bytes 11796484
  122.3 1.2 copy-start.4
  123.5 7.5 %collective-permute-start.11 = (f32[256,2560]{1,0:T(8,128)S(1)}, f32[256,2560]{1,0:T(8,128)}, u32[]{:S(2)}, u32[]{:S(2)}) collective-permute-start(f32[256,2560]{1,0:T(8,128)S(1)} %fusion.39), channel_id=1, source_target_pairs={{0,1},{1,0},{2,3},{3,2},{4,5},{5,4},{6,7},{7,6},{8,9},{9,8},{10,11... | collective-permute-start | bytes 7864328 | tf_op jit(solution)/shard_map/ppermute | solution.py:161
  124.8 6.2 %copy-start.3 = (bf16[2560,768]{1,0:T(8,128)(2,1)S(1)}, bf16[2560,768]{1,0:T(8,128)(2,1)}, u32[]{:S(2)}) copy-start(bf16[2560,768]{1,0:T(8,128)(2,1)} %param.8) | copy-start | bytes 11796484
  124.8 6.2 %copy-start.5 = (bf16[512,768]{1,0:T(8,128)(2,1)S(1)}, bf16[512,768]{1,0:T(8,128)(2,1)}, u32[]{:S(2)}) copy-start(bf16[512,768]{1,0:T(8,128)(2,1)} %copy-done.4) | copy-start | bytes 2359300
